TPU v7x, 32 devices: a whole 2x2x4 slice. The times are simulated.
32 devices in a mesh: req: 8 (over z, x), tp: 4 (over y, core).
Axes of the slice: x: 2, y: 2, z: 4, core: 2. Of those that a mesh axis runs over, the one named last changes fastest.
Arguments:
- tokens: bfloat16 [4096, 2048], P('req', 'tp'), may hold values from -6 to 6
- first_gain: float32 [2048], replicated, may hold values from 0.5 to 1.5
- first_shift: float32 [2048], replicated, may hold values from -2.5 to 2.5
- project_weight: bfloat16 [2048, 3, 2048], P(None, None, 'tp'), may hold values from -0.125 to 0.125
- project_bias: float32 [3, 2048], P(None, 'tp'), may hold values from -3 to 3
- output_weight: bfloat16 [2048, 2048], P('tp'), may hold values from -0.125 to 0.125
- second_gain: float32 [2048], replicated, may hold values from 0.5 to 1.5
- second_shift: float32 [2048], replicated, may hold values from -2.5 to 2.5
- expand_weight: bfloat16 [2048, 2, 3072], P(None, None, 'tp'), may hold values from -0.125 to 0.125
- contract_weight: bfloat16 [3072, 2048], P('tp'), may hold values from -0.109375 to 0.109375
- prior_cache: bfloat16 [8, 1024, 2, 2048], P('req', None, None, 'tp'), may hold values from -21 to 21
- prior_len: int32 [8], replicated, may hold values from 16 to 1024, as said below
- slot_map: int32 [8], replicated, may hold values from 0 to 7, each once
- block_table: int32 [8, 6], replicated, may hold values from 0 to 11, as said below
Outputs:
- mixed_out: bfloat16 [4096, 2048], P('req', 'tp')
- page_pool: bfloat16 [8, 12, 256, 2, 1024], P('req', None, None, None, 'tp')
Inputs may be any that keep to these rules, and one draw needn't show every extreme that they name: `prior_len`: every request has at least 16 cached positions; some request has exactly 1024. `block_table`: rows 2g and 2g+1 together name each of the 12 pages exactly once.
All inputs are finite; a program needn't handle non-finite values.
Results may differ from a plain program's by a relative error of at most 0.018.
Values may be sent and summed in bfloat16 or wider, within the bound.
A program may use at most 128 MiB of HBM per device.

v0:
```python
import jax
import jax.numpy as jnp
from jax import lax
from jax.experimental import pallas as pl
from jax.experimental.pallas import tpu as pltpu
from jax.sharding import PartitionSpec as P

HEAD_DIM = 64
ROTARY = 16
BLOCK = 256


EPSILON = 1e-05
ROPE_BASE = 10000.0
MASK_FILL = -1e30


def layer_norm(inputs, gain_row, shift_row):
    center = inputs - jnp.mean(inputs, axis=-1, keepdims=True)
    spread = jnp.mean(center * center, axis=-1, keepdims=True)
    return (center * lax.rsqrt(spread + EPSILON) * gain_row + shift_row).astype(jnp.bfloat16)


def rotate(values, positions):
    half_rot = ROTARY // 2
    frequency = ROPE_BASE ** (-2.0 * jnp.arange(half_rot, dtype=jnp.float32) / ROTARY)
    angles = positions.astype(jnp.float32)[:, None] * frequency[None, :]
    cosine = jnp.cos(angles)[:, None, :]
    sine_part = jnp.sin(angles)[:, None, :]
    first_half = values[..., :half_rot]
    second_half = values[..., half_rot:ROTARY]
    return jnp.concatenate(
        [
            first_half * cosine - second_half * sine_part,
            second_half * cosine + first_half * sine_part,
            values[..., ROTARY:],
        ],
        axis=-1,
    )


def attend(queries, key_rows, value_rows, prior_count):
    query_count = queries.shape[0]
    cache_rows = key_rows.shape[0] - query_count
    scores = jnp.einsum(
        "qhd,khd->hqk", queries, key_rows, preferred_element_type=jnp.float32
    ) * HEAD_DIM ** (-0.5)
    key_index = jnp.arange(key_rows.shape[0], dtype=jnp.int32)[None, :]
    query_index = jnp.arange(query_count, dtype=jnp.int32)[:, None]
    allowed = jnp.where(
        key_index < cache_rows, key_index < prior_count, key_index - cache_rows <= query_index
    )
    scores = jnp.where(allowed[None], scores, MASK_FILL)
    highest = jnp.max(scores, axis=-1, keepdims=True)
    weights = jnp.exp(scores - highest)
    normalized = (weights / jnp.sum(weights, axis=-1, keepdims=True)).astype(jnp.bfloat16)
    mixture = jnp.einsum("hqk,khd->qhd", normalized, value_rows, preferred_element_type=jnp.float32)
    return mixture.astype(jnp.bfloat16)


def regroup(pieces, by_slot):
    count, span_len, _, width = pieces.shape
    half_width = width // 2

    def kernel(by_slot_ref, pieces_ref, out_ref, sems):
        copies = []
        for device in range(count):
            for slot in range(2):
                source = by_slot_ref[2 * (device // 2) + slot]
                columns = pl.ds((device % 2) * half_width, half_width)
                copies.append(
                    pltpu.make_async_copy(
                        pieces_ref.at[source, :, :, columns],
                        out_ref.at[device, slot],
                        sems.at[2 * device + slot],
                    )
                )
                copies[-1].start()
        for copy in copies:
            copy.wait()

    return pl.pallas_call(
        kernel,
        out_shape=jax.ShapeDtypeStruct((count, 2, span_len, 2, half_width), pieces.dtype),
        in_specs=[pl.BlockSpec(memory_space=pltpu.SMEM), pl.BlockSpec(memory_space=pl.ANY)],
        out_specs=pl.BlockSpec(memory_space=pl.ANY),
        scratch_shapes=[pltpu.SemaphoreType.DMA((2 * count,))],
        cost_estimate=pl.CostEstimate(flops=0, bytes_accessed=4 * pieces.size, transcendentals=0),
        name="regroup",
    )(by_slot, pieces)


def place_pages(prior_rows, new_rows, lengths, pages):
    count, _, prior_span, _, width = prior_rows.shape
    new_span = new_rows.shape[2]
    prior_total, new_total = count * prior_span, count * new_span
    blocks = (prior_total + new_total) // BLOCK
    tail = prior_total // BLOCK

    def kernel(lengths_ref, pages_ref, prior_ref, new_ref, zero_ref, pool_ref, rows, *sems):
        prior_sems, new_sems, zero_sems, page_sems = sems
        copies = []
        for slot in range(2):
            for piece in range(count):
                copies.append(
                    pltpu.make_async_copy(
                        prior_ref.at[piece, slot],
                        rows.at[slot, pl.ds(piece * prior_span, prior_span)],
                        prior_sems.at[slot * count + piece],
                    )
                )
                copies[-1].start()
        for copy in copies:
            copy.wait()
        copies = []
        for slot in range(2):
            length = lengths_ref[slot]
            for piece in range(count):
                copies.append(
                    pltpu.make_async_copy(
                        new_ref.at[piece, slot],
                        rows.at[slot, pl.ds(length + piece * new_span, new_span)],
                        new_sems.at[slot * count + piece],
                    )
                )
                copies[-1].start()
            for piece in range(tail):
                copies.append(
                    pltpu.make_async_copy(
                        zero_ref,
                        rows.at[slot, pl.ds(length + new_total + piece * BLOCK, BLOCK)],
                        zero_sems.at[slot * tail + piece],
                    )
                )
                copies[-1].start()
        for copy in copies:
            copy.wait()
        copies = []
        for slot in range(2):
            for block in range(blocks):
                copies.append(
                    pltpu.make_async_copy(
                        rows.at[slot, pl.ds(block * BLOCK, BLOCK)],
                        pool_ref.at[pages_ref[slot * blocks + block]],
                        page_sems.at[slot * blocks + block],
                    )
                )
                copies[-1].start()
        for copy in copies:
            copy.wait()

    return pl.pallas_call(
        kernel,
        out_shape=jax.ShapeDtypeStruct((2 * blocks, BLOCK, 2, width), prior_rows.dtype),
        in_specs=[pl.BlockSpec(memory_space=pltpu.SMEM)] * 2
        + [pl.BlockSpec(memory_space=pl.ANY)] * 3,
        out_specs=pl.BlockSpec(memory_space=pl.ANY),
        scratch_shapes=[
            pltpu.VMEM((2, 2 * prior_total + new_total, 2, width), prior_rows.dtype),
            pltpu.SemaphoreType.DMA((2 * count,)),
            pltpu.SemaphoreType.DMA((2 * count,)),
            pltpu.SemaphoreType.DMA((2 * tail,)),
            pltpu.SemaphoreType.DMA((2 * blocks,)),
        ],
        compiler_params=pltpu.CompilerParams(vmem_limit_bytes=48 * 1024 * 1024),
        cost_estimate=pl.CostEstimate(
            flops=0, bytes_accessed=4 * (prior_rows.size + new_rows.size), transcendentals=0
        ),
        name="place_pages",
    )(lengths, pages, prior_rows, new_rows, jnp.zeros((BLOCK, 2, width), prior_rows.dtype))


NEAR = [(0, 1), (1, 0), (2, 3), (3, 2)]
FAR = [(0, 2), (2, 0), (1, 3), (3, 1)]


def gather_columns(share):
    me = lax.axis_index("tp")
    odd, high = me % 2 == 1, me >= 2
    far = lax.ppermute(share, "tp", FAR)
    near = lax.ppermute(share, "tp", NEAR)
    far_near = lax.ppermute(far, "tp", NEAR)
    own_first, own_second = jnp.where(odd, near, share), jnp.where(odd, share, near)
    far_first, far_second = jnp.where(odd, far_near, far), jnp.where(odd, far, far_near)
    return jnp.concatenate(
        [
            jnp.where(high, far_first, own_first),
            jnp.where(high, far_second, own_second),
            jnp.where(high, own_first, far_first),
            jnp.where(high, own_second, far_second),
        ],
        axis=1,
    )


def scatter_sum(partial):
    me = lax.axis_index("tp")
    odd, high = me % 2 == 1, me >= 2
    width = partial.shape[1] // 4
    blocks = [partial[:, at * width : (at + 1) * width] for at in range(4)]

    def near_sum(even_block, odd_block):
        received = lax.ppermute(jnp.where(odd, even_block, odd_block), "tp", NEAR)
        return jnp.where(odd, odd_block, even_block).astype(jnp.float32) + received.astype(
            jnp.float32
        )

    low_half = near_sum(blocks[0], blocks[1])
    high_half = near_sum(blocks[2], blocks[3])
    leaving = jnp.where(high, low_half, high_half).astype(jnp.bfloat16)
    received = lax.ppermute(leaving, "tp", FAR)
    return jnp.where(high, high_half, low_half) + received.astype(jnp.float32)


def local(
    tokens,
    first_gain,
    first_shift,
    project_weight,
    project_bias,
    output_weight,
    second_gain,
    second_shift,
    expand_weight,
    contract_weight,
    prior_cache,
    prior_len,
    slot_map,
    block_table,
):
    request = lax.axis_index("req")
    prior_count = prior_len[request]
    stretch_len = tokens.shape[0]
    local_width = project_weight.shape[2]
    local_heads = local_width // HEAD_DIM
    local_hidden = expand_weight.shape[2]
    cached = prior_cache[0]
    req_count = slot_map.shape[0]
    cache_len = cached.shape[0]
    by_slot = jnp.sum(
        jnp.where(
            slot_map[None, :] == jnp.arange(req_count, dtype=jnp.int32)[:, None],
            jnp.arange(req_count, dtype=jnp.int32)[None, :],
            0,
        ),
        axis=1,
    )
    prior_pieces = lax.all_to_all(
        cached.reshape(req_count, cache_len // req_count, 2, local_width),
        "req",
        split_axis=0,
        concat_axis=0,
        tiled=True,
    )
    prior_received = lax.all_to_all(
        regroup(prior_pieces, by_slot), "req", split_axis=0, concat_axis=0, tiled=True
    )
    token_rows = gather_columns(tokens)
    inputs = token_rows.astype(jnp.float32)
    normed = layer_norm(inputs, first_gain, first_shift)
    projected = (
        jnp.dot(
            normed,
            project_weight.reshape(project_weight.shape[0], 3 * local_width),
            preferred_element_type=jnp.float32,
        ).reshape(stretch_len, 3, local_width)
        + project_bias
    )
    positions = prior_count + jnp.arange(stretch_len, dtype=jnp.int32)
    queries = rotate(projected[:, 0].reshape(stretch_len, local_heads, HEAD_DIM), positions).astype(
        jnp.bfloat16
    )
    new_keys = rotate(
        projected[:, 1].reshape(stretch_len, local_heads, HEAD_DIM), positions
    ).astype(jnp.bfloat16)
    new_values = projected[:, 2].reshape(stretch_len, local_heads, HEAD_DIM).astype(jnp.bfloat16)
    key_rows = jnp.concatenate(
        [cached[:, 0].reshape(cache_len, local_heads, HEAD_DIM), new_keys], axis=0
    )
    value_rows = jnp.concatenate(
        [cached[:, 1].reshape(cache_len, local_heads, HEAD_DIM), new_values], axis=0
    )
    mixture = attend(queries, key_rows, value_rows, prior_count).reshape(stretch_len, local_width)
    partial_value = jnp.dot(mixture, output_weight, preferred_element_type=jnp.float32)
    mixer_share = scatter_sum(partial_value.astype(jnp.bfloat16))
    residual_share = (tokens.astype(jnp.float32) + mixer_share).astype(jnp.bfloat16)
    residual = gather_columns(residual_share)
    second_normed = layer_norm(residual.astype(jnp.float32), second_gain, second_shift)
    gate_up = jnp.dot(
        second_normed,
        expand_weight.reshape(expand_weight.shape[0], 2 * local_hidden),
        preferred_element_type=jnp.float32,
    ).reshape(stretch_len, 2, local_hidden)
    hidden = (jax.nn.silu(gate_up[:, 0]) * gate_up[:, 1]).astype(jnp.bfloat16)
    down_share = scatter_sum(
        jnp.dot(hidden, contract_weight, preferred_element_type=jnp.float32).astype(jnp.bfloat16)
    )
    result = (residual_share.astype(jnp.float32) + down_share).astype(jnp.bfloat16)
    fresh_cache = jnp.stack(
        [new_keys.reshape(stretch_len, local_width), new_values.reshape(stretch_len, local_width)],
        axis=1,
    )
    new_pieces = lax.all_to_all(
        fresh_cache.reshape(req_count, stretch_len // req_count, 2, local_width),
        "req",
        split_axis=0,
        concat_axis=0,
        tiled=True,
    )
    new_received = lax.all_to_all(
        regroup(new_pieces, by_slot), "req", split_axis=0, concat_axis=0, tiled=True
    )
    group_index = request // 2
    slots = lax.dynamic_slice_in_dim(by_slot, 2 * group_index, 2, 0)
    lengths = jnp.take(prior_len, slots)
    pages = lax.dynamic_slice_in_dim(block_table, 2 * group_index, 2, 0).reshape(-1)
    page_pool = place_pages(prior_received, new_received, lengths, pages)[None]
    return (result, page_pool)


def solution(mesh):
    return jax.shard_map(
        local,
        mesh=mesh,
        in_specs=(
            P("req", "tp"),
            P(),
            P(),
            P(None, None, "tp"),
            P(None, "tp"),
            P("tp", None),
            P(),
            P(),
            P(None, None, "tp"),
            P("tp", None),
            P("req", None, None, "tp"),
            P(),
            P(),
            P(),
        ),
        out_specs=(P("req", "tp"), P("req", None, None, None, "tp")),
        check_vma=False,
    )
```

profile of v0, /device:TPU:0, one launch (start us, length us, event | category | flops | bytes accessed | tf_op | source)
XLA Modules:
  0.0 320.1 jit_solution(13265472162511012436)
XLA Ops:
  3.7 12.2 %collective-permute-done = bf16[512,512]{1,0:T(8,128)(2,1)} collective-permute-done((bf16[512,512]{1,0:T(8,128)(2,1)}, bf16[512,512]{1,0:T(8,128)(2,1)}, u32[]{:S(2)}, u32[]{:S(2)}) %collective-permute-start) | collective-permute-done | bytes 524320 | tf_op jit(solution)/shard_map/ppermute | solution.py:180
  15.9 8.8 %copy.30 = bf16[2048,3,512]{0,2,1:T(8,128)(2,1)} copy(bf16[2048,3,512]{2,0,1:T(8,128)(2,1)} %param.17) | data formatting | bytes 12582912 | tf_op args[3]
  29.6 3.7 %fusion.34 = f32[512,3,512]{0,2,1:T(8,128)S(1)} fusion(bf16[2048,3,512]{0,2,1:T(8,128)(2,1)S(1)} %copy-done.3, f32[2048]{0:T(1024)S(1)} %copy-done.12, f32[2048]{0:T(1024)S(1)} %copy-done.13, f32[512]{0:T(512)S(1)} %add_rsqrt_fusion.1, f32[512]{0:T(512)S(1)} %broadcast_multiply_fusion.1, f32[3,512]{1,0:T(4,128)S(1)} %copy-done.14, ...), kind=kOutput, calls=%fused_computation.45 | convolution fusion | flops 3235643392 | bytes 11560960 | tf_op jit(solution)/shard_map/dot_general | solution.py:262
  38.6 4.2 %copy.35 = bf16[8,64,1,512]{3,2,1,0:T(2,128)(2,1)} copy(bf16[8,64,1,512]{1,0,3,2:T(8,128)(2,1)} %reshape.209) | data formatting | bytes 1048576 | tf_op jit(solution)/shard_map/convert_element_type | solution.py:275
  46.8 4.3 %pad_maximum_fusion.2 = bf16[8,64,2,512]{3,2,1,0:T(2,128)(2,1)} fusion(bf16[8,64,1,512]{3,2,1,0:T(2,128)(2,1)S(1)} %copy.36, bf16[8,64,1,512]{3,2,1,0:T(2,128)(2,1)} %copy.35), kind=kLoop, calls=%fused_computation.62 | loop fusion | flops 2097152 | bytes 2097152 | tf_op jit(solution)/shard_map/stack | solution.py:299
  51.1 6.0 %all-to-all-start.2 = ((bf16[8,64,2,512]{3,2,1,0:T(2,128)(2,1)}), bf16[8,64,2,512]{3,2,1,0:T(2,128)(2,1)}, u32[]{:S(2)}, u32[]{:S(2)}) async-start(bf16[8,64,2,512]{3,2,1,0:T(2,128)(2,1)} %pad_maximum_fusion.2), calls=%async_computation.2 | async-start | bytes 2097152 | tf_op jit(solution)/shard_map/all_to_all | solution.py:303
  57.1 6.9 %fusion.82 = (bf16[1024,1,512]{2,1,0:T(2,128)(2,1)}, bf16[1024,1,512]{2,1,0:T(2,128)(2,1)}) fusion(bf16[1024,2,512]{2,1,0:T(2,128)(2,1)} %bitcast.54), kind=kLoop, calls=%fused_computation.129 | loop fusion | bytes 4194304 | tf_op jit(solution)/shard_map/slice | solution.py:281
  64.0 5.8 %copy.29 = bf16[1024,1,512]{0,2,1:T(8,128)(2,1)} copy(bf16[1024,1,512]{2,1,0:T(2,128)(2,1)} %get-tuple-element.12) | data formatting | bytes 2097152 | tf_op jit(solution)/shard_map/slice | solution.py:281
  69.8 5.8 %copy.31 = bf16[1024,1,512]{0,2,1:T(8,128)(2,1)} copy(bf16[1024,1,512]{2,1,0:T(2,128)(2,1)} %get-tuple-element.13) | data formatting | bytes 2097152 | tf_op jit(solution)/shard_map/slice | solution.py:278
  83.7 4.5 %all-to-all-start = ((bf16[8,128,2,512]{3,2,1,0:T(2,128)(2,1)}), bf16[8,128,2,512]{3,2,1,0:T(2,128)(2,1)}, u32[]{:S(2)}, u32[]{:S(2)}) async-start(bf16[8,128,2,512]{3,2,1,0:T(2,128)(2,1)} %bitcast.55), calls=%async_computation | async-start | bytes 4194304 | tf_op jit(solution)/shard_map/all_to_all | solution.py:248
  88.2 10.6 %fusion.83 = f32[8,512]{1,0:T(8,128)} fusion(pred[512,1536]{1,0:T(8,128)(4,1)} %fusion.20, bf16[512,8,64]{0,2,1:T(8,128)(2,1)} %maximum_convert_fusion, bf16[1024,8,64]{0,2,1:T(8,128)(2,1)} %bitcast.66, bf16[512,8,48]{0,2,1:T(8,128)(2,1)S(1)} %slice.177, bf16[512,8,8]{0,2,1:T(8,128)(2,1)} %get-tuple-element.19, bf16[512,8,8]{0,2,1:T(8,128)(2,1)} %get-tuple-element.18), kind=kOutput, calls=%fused_computation.130 | convolution fusion | flops 835192320 | bytes 2899968 | tf_op jit(solution)/shard_map/sub | solution.py:55
  98.9 12.0 %fusion.58 = bf16[8,64,512]{2,1,0:T(8,128)(2,1)} fusion(f32[8,512]{1,0:T(8,128)} %fusion.83, bf16[512,8,64]{0,2,1:T(8,128)(2,1)} %bitcast.64, bf16[1024,8,64]{0,2,1:T(8,128)(2,1)} %bitcast.65, pred[512,1536]{1,0:T(8,128)(4,1)} %fusion.20, bf16[512,8,64]{0,2,1:T(8,128)(2,1)} %maximum_convert_fusion, bf16[1024,8,64]{0,2,1:T(8,128)(2,1)} %bitcast.67, ...), kind=kOutput, calls=%fused_computation.59 | convolution fusion | flops 1650202112 | bytes 4997120 | tf_op jit(solution)/shard_map/hqk,khd->qhd/dot_general | solution.py:57
  118.7 12.5 %collective-permute-done.5 = bf16[512,512]{1,0:T(8,128)(2,1)S(1)} collective-permute-done((bf16[512,512]{1,0:T(8,128)(2,1)S(1)}, bf16[512,512]{1,0:T(8,128)(2,1)S(1)}, u32[]{:S(2)}, u32[]{:S(2)}) %collective-permute-start.5) | collective-permute-done | bytes 524320 | tf_op jit(solution)/shard_map/ppermute | solution.py:211
  134.7 33.7 %regroup.3 = bf16[8,2,64,2,256]{4,3,2,1,0:T(2,128)(2,1)} custom-call(s32[8]{0:T(128)} %select_reduce_fusion.by_slot_ref, bf16[8,64,2,512]{3,2,1,0:T(2,128)(2,1)} %all-to-all-done.2.pieces_ref), custom_call_target="tpu_custom_call" | custom-call | bytes 2097152 | tf_op jit(solution)/shard_map/regroup/pallas_call | solution.py:82
  168.4 5.7 %all-to-all-start.3 = ((bf16[8,2,64,2,256]{4,3,2,1,0:T(2,128)(2,1)}), bf16[8,2,64,2,256]{4,3,2,1,0:T(2,128)(2,1)}, u32[]{:S(2)}, u32[]{:S(2)}) async-start(bf16[8,2,64,2,256]{4,3,2,1,0:T(2,128)(2,1)} %regroup.3), calls=%async_computation.3 | async-start | bytes 2097152 | tf_op jit(solution)/shard_map/all_to_all | solution.py:310
  174.7 6.8 %copy.39 = bf16[256,8,2,768]{3,1,2,0:T(8,128)(2,1)} copy(bf16[256,8,2,768]{3,2,1,0:T(2,128)(2,1)} %bitcast.56) | data formatting | bytes 12582912
  181.4 8.7 %copy.32 = bf16[1536,2048]{1,0:T(8,128)(2,1)} copy(bf16[1536,2048]{0,1:T(8,128)(2,1)} %bitcast.53) | data formatting | bytes 12582912 | tf_op jit(solution)/shard_map/dot_general | solution.py:289
  194.1 65.6 %regroup.2 = bf16[8,2,128,2,256]{4,3,2,1,0:T(2,128)(2,1)} custom-call(s32[8]{0:T(128)} %select_reduce_fusion.by_slot_ref, bf16[8,128,2,512]{3,2,1,0:T(2,128)(2,1)} %all-to-all-done.pieces_ref), custom_call_target="tpu_custom_call" | custom-call | bytes 4194304 | tf_op jit(solution)/shard_map/regroup/pallas_call | solution.py:82
  259.7 6.0 %all-to-all-start.1 = ((bf16[8,2,128,2,256]{4,3,2,1,0:T(2,128)(2,1)}), bf16[8,2,128,2,256]{4,3,2,1,0:T(2,128)(2,1)}, u32[]{:S(2)}, u32[]{:S(2)}) async-start(bf16[8,2,128,2,256]{4,3,2,1,0:T(2,128)(2,1)} %regroup.2), calls=%async_computation.1 | async-start | bytes 4194304 | tf_op jit(solution)/shard_map/all_to_all | solution.py:255
  265.8 7.0 %fusion.24 = f32[512,2,768]{2,0,1:T(8,128)S(1)} fusion(bf16[2,768,2048]{2,1,0:T(8,128)(2,1)} %bitcast.57, f32[2048]{0:T(1024)S(1)} %copy-done.15, f32[2048]{0:T(1024)S(1)} %copy-done.16, f32[512]{0:T(512)S(1)} %add_rsqrt_fusion, f32[512]{0:T(512)S(1)} %broadcast_multiply_fusion, bf16[512,512]{1,0:T(8,128)(2,1)} %copy-done.7, ...), kind=kOutput, calls=%fused_computation.34 | convolution fusion | flops 3234856960 | bytes 11554816 | tf_op jit(solution)/shard_map/dot_general | solution.py:289
  285.3 12.2 %collective-permute-done.11 = bf16[512,512]{1,0:T(8,128)(2,1)} collective-permute-done((bf16[512,512]{1,0:T(8,128)(2,1)}, bf16[512,512]{1,0:T(8,128)(2,1)}, u32[]{:S(2)}, u32[]{:S(2)}) %collective-permute-start.11) | collective-permute-done | bytes 524320 | tf_op jit(solution)/shard_map/ppermute | solution.py:211
  297.4 3.5 %add_convert_fusion = bf16[512,512]{1,0:T(8,128)(2,1)} fusion(bf16[512,512]{1,0:T(8,128)(2,1)} %collective-permute-done.11, bf16[512,512]{1,0:T(8,128)(2,1)} %add_convert_fusion.1, bf16[512,512]{1,0:T(8,128)(2,1)} %collective-permute-done.9, bf16[512,512]{1,0:T(8,128)(2,1)} %collective-permute-done.10, pred[]{:T(512)S(6)} %ge.11, ...), kind=kLoop, calls=%fused_computation.63 | loop fusion | flops 3670016 | bytes 4718594 | tf_op jit(solution)/shard_map/convert_element_type | solution.py:298
  300.9 13.4 %all-to-all-done.1.prior_ref = bf16[8,2,128,2,256]{4,3,2,1,0:T(2,128)(2,1)} async-done(((bf16[8,2,128,2,256]{4,3,2,1,0:T(2,128)(2,1)}), bf16[8,2,128,2,256]{4,3,2,1,0:T(2,128)(2,1)}, u32[]{:S(2)}, u32[]{:S(2)}) %all-to-all-start.1) | async-done | bytes 2097184 | tf_op jit(solution)/shard_map/all_to_all | solution.py:255
  314.5 5.5 %place_pages.1 = bf16[12,256,2,256]{3,2,1,0:T(2,128)(2,1)} custom-call(s32[2]{0:T(128)S(1)} %and_select_fusion.lengths_ref, s32[12]{0:T(128)S(1)} %reshape.197.pages_ref, bf16[8,2,128,2,256]{4,3,2,1,0:T(2,128)(2,1)} %all-to-all-done.1.prior_ref, bf16[8,2,64,2,256]{4,3,2,1,0:T(2,128)(2,1)} %all-to-all-done.3.new_ref, ...), custom_call_target="tpu_custom_call" | custom-call | bytes 6291456 | tf_op jit(solution)/shard_map/place_pages/pallas_call | solution.py:152
  (102 shorter events, 53.5 us)
Async XLA Ops:
  0.6 272.2 %copy-start = (bf16[768,2048]{1,0:T(8,128)(2,1)S(1)}, bf16[768,2048]{1,0:T(8,128)(2,1)}, u32[]{:S(2)}) copy-start(bf16[768,2048]{1,0:T(8,128)(2,1)} %param.23) | copy-start | bytes 9437188
  0.6 15.3 %collective-permute-start = (bf16[512,512]{1,0:T(8,128)(2,1)}, bf16[512,512]{1,0:T(8,128)(2,1)}, u32[]{:S(2)}, u32[]{:S(2)}) collective-permute-start(bf16[512,512]{1,0:T(8,128)(2,1)} %param.14), channel_id=1, source_target_pairs={{0,2},{2,0},{1,3},{3,1},{4,6},{6,4},{5,7},{7,5},{8,10},{10,8},{9,1... | collective-permute-start | bytes 1572872 | tf_op jit(solution)/shard_map/ppermute | solution.py:180
  3.7 22.6 %collective-permute-start.2 = (bf16[512,512]{1,0:T(8,128)(2,1)}, bf16[512,512]{1,0:T(8,128)(2,1)}, u32[]{:S(2)}, u32[]{:S(2)}) collective-permute-start(bf16[512,512]{1,0:T(8,128)(2,1)} %param.14), channel_id=1, source_target_pairs={{0,1},{1,0},{2,3},{3,2},{4,5},{5,4},{6,7},{7,6},{8,9},{9,8},{10,11... | collective-permute-start | bytes 1572872 | tf_op jit(solution)/shard_map/ppermute | solution.py:181
  15.9 10.3 %collective-permute-start.1 = (bf16[512,512]{1,0:T(8,128)(2,1)}, bf16[512,512]{1,0:T(8,128)(2,1)}, u32[]{:S(2)}, u32[]{:S(2)}) collective-permute-start(bf16[512,512]{1,0:T(8,128)(2,1)} %collective-permute-done), channel_id=1, source_target_pairs={{0,1},{1,0},{2,3},{3,2},{4,5},{5,4},{6,7},{7,6},{8,9},{9,8},{10,11... | collective-permute-start | bytes 1572872 | tf_op jit(solution)/shard_map/ppermute | solution.py:182
  15.9 8.8 %copy-start.1 = (s32[8]{0:T(128)S(1)}, s32[8]{0:T(128)}, u32[]{:S(2)}) copy-start(s32[8]{0:T(128)} %param.25) | copy-start | bytes 100
  26.2 9.2 %copy-start.9 = (f32[512,8]{0,1:T(8,128)}, f32[512,8]{0,1:T(8,128)S(1)}, u32[]{:S(2)}) copy-start(f32[512,8]{0,1:T(8,128)S(1)} %get-tuple-element.22) | copy-start | bytes 49156
  26.2 9.2 %copy-start.10 = (f32[512,8]{0,1:T(8,128)}, f32[512,8]{0,1:T(8,128)S(1)}, u32[]{:S(2)}) copy-start(f32[512,8]{0,1:T(8,128)S(1)} %get-tuple-element.23) | copy-start | bytes 49156
  51.1 32.6 %all-to-all-start.2 = ((bf16[8,64,2,512]{3,2,1,0:T(2,128)(2,1)}), bf16[8,64,2,512]{3,2,1,0:T(2,128)(2,1)}, u32[]{:S(2)}, u32[]{:S(2)}) async-start(bf16[8,64,2,512]{3,2,1,0:T(2,128)(2,1)} %pad_maximum_fusion.2), calls=%async_computation.2 | async-start | bytes 2097152 | tf_op jit(solution)/shard_map/all_to_all | solution.py:303
  83.7 84.8 %all-to-all-start = ((bf16[8,128,2,512]{3,2,1,0:T(2,128)(2,1)}), bf16[8,128,2,512]{3,2,1,0:T(2,128)(2,1)}, u32[]{:S(2)}, u32[]{:S(2)}) async-start(bf16[8,128,2,512]{3,2,1,0:T(2,128)(2,1)} %bitcast.55), calls=%async_computation | async-start | bytes 4194304 | tf_op jit(solution)/shard_map/all_to_all | solution.py:248
  113.9 17.3 %copy-start.8 = (bf16[512,512]{1,0:T(8,128)(2,1)S(1)}, bf16[512,512]{1,0:T(8,128)(2,1)}, u32[]{:S(2)}) copy-start(bf16[512,512]{1,0:T(8,128)(2,1)} %param.14) | copy-start | bytes 1572868
  114.0 2.0 collective-permute-start.4
  114.1 19.9 %copy-start.17 = (s32[8]{0:T(128)S(1)}, s32[8]{0:T(128)}, u32[]{:S(2)}) copy-start(s32[8]{0:T(128)} %param.26) | copy-start | bytes 100
  114.1 2.6 collective-permute-start.3
  117.1 14.0 %collective-permute-start.5 = (bf16[512,512]{1,0:T(8,128)(2,1)S(1)}, bf16[512,512]{1,0:T(8,128)(2,1)S(1)}, u32[]{:S(2)}, u32[]{:S(2)}) collective-permute-start(bf16[512,512]{1,0:T(8,128)(2,1)S(1)} %select_convert_fusion.1), channel_id=1, source_target_pairs={{0,2},{2,0},{1,3},{3,1},{4,6},{6,4},{5,7},{7,5},{8,10},{10,8},{9,1... | collective-permute-start | bytes 1572872 | tf_op jit(solution)/shard_map/ppermute | solution.py:211
  132.5 41.6 %collective-permute-start.6 = (bf16[512,512]{1,0:T(8,128)(2,1)}, bf16[512,512]{1,0:T(8,128)(2,1)}, u32[]{:S(2)}, u32[]{:S(2)}) collective-permute-start(bf16[512,512]{1,0:T(8,128)(2,1)} %add_convert_fusion.1), channel_id=1, source_target_pairs={{0,2},{2,0},{1,3},{3,1},{4,6},{6,4},{5,7},{7,5},{8,10},{10,8},{9,1... | collective-permute-start | bytes 1572872 | tf_op jit(solution)/shard_map/ppermute | solution.py:180
  168.4 91.3 %all-to-all-start.3 = ((bf16[8,2,64,2,256]{4,3,2,1,0:T(2,128)(2,1)}), bf16[8,2,64,2,256]{4,3,2,1,0:T(2,128)(2,1)}, u32[]{:S(2)}, u32[]{:S(2)}) async-start(bf16[8,2,64,2,256]{4,3,2,1,0:T(2,128)(2,1)} %regroup.3), calls=%async_computation.3 | async-start | bytes 2097152 | tf_op jit(solution)/shard_map/all_to_all | solution.py:310
  174.1 16.0 %collective-permute-start.8 = (bf16[512,512]{1,0:T(8,128)(2,1)}, bf16[512,512]{1,0:T(8,128)(2,1)}, u32[]{:S(2)}, u32[]{:S(2)}) collective-permute-start(bf16[512,512]{1,0:T(8,128)(2,1)} %add_convert_fusion.1), channel_id=1, source_target_pairs={{0,1},{1,0},{2,3},{3,2},{4,5},{5,4},{6,7},{7,6},{8,9},{9,8},{10,11... | collective-permute-start | bytes 1572872 | tf_op jit(solution)/shard_map/ppermute | solution.py:181
  174.2 16.0 %collective-permute-start.7 = (bf16[512,512]{1,0:T(8,128)(2,1)}, bf16[512,512]{1,0:T(8,128)(2,1)}, u32[]{:S(2)}, u32[]{:S(2)}) collective-permute-start(bf16[512,512]{1,0:T(8,128)(2,1)} %collective-permute-done.6), channel_id=1, source_target_pairs={{0,1},{1,0},{2,3},{3,2},{4,5},{5,4},{6,7},{7,6},{8,9},{9,8},{10,11... | collective-permute-start | bytes 1572872 | tf_op jit(solution)/shard_map/ppermute | solution.py:182
  194.1 71.6 %copy-start.15 = (f32[2048]{0:T(1024)S(1)}, f32[2048]{0:T(1024)}, u32[]{:S(2)}) copy-start(f32[2048]{0:T(1024)} %param.21) | copy-start | bytes 24580
  194.1 71.6 %copy-start.16 = (f32[2048]{0:T(1024)S(1)}, f32[2048]{0:T(1024)}, u32[]{:S(2)}) copy-start(f32[2048]{0:T(1024)} %param.20) | copy-start | bytes 24580
  259.7 54.6 %all-to-all-start.1 = ((bf16[8,2,128,2,256]{4,3,2,1,0:T(2,128)(2,1)}), bf16[8,2,128,2,256]{4,3,2,1,0:T(2,128)(2,1)}, u32[]{:S(2)}, u32[]{:S(2)}) async-start(bf16[8,2,128,2,256]{4,3,2,1,0:T(2,128)(2,1)} %regroup.2), calls=%async_computation.1 | async-start | bytes 4194304 | tf_op jit(solution)/shard_map/all_to_all | solution.py:255
  277.1 2.3 collective-permute-start.10
  277.1 3.0 collective-permute-start.9
  283.2 14.3 %collective-permute-start.11 = (bf16[512,512]{1,0:T(8,128)(2,1)}, bf16[512,512]{1,0:T(8,128)(2,1)}, u32[]{:S(2)}, u32[]{:S(2)}) collective-permute-start(bf16[512,512]{1,0:T(8,128)(2,1)} %select_convert_fusion), channel_id=1, source_target_pairs={{0,2},{2,0},{1,3},{3,1},{4,6},{6,4},{5,7},{7,5},{8,10},{10,8},{9,1... | collective-permute-start | bytes 1572872 | tf_op jit(solution)/shard_map/ppermute | solution.py:211
  (10 other events, 27.7 us)
where the time goes:
time: 322 us; the launch traced here: 320 us
  Pallas kernels  105 us (33%)
  local copies, waits for them, and re-layouts  61.4 us (19%)
  waiting for transfers between devices  58 us (18%)
  matrix products  38.2 us (12%)
  starting transfers between devices  30.5 us (9%)
  other arithmetic  26.2 us (8%)
    pallas_call x2, Pallas kernels, regroup(): pl.pallas_call(kernel, out_shape=jax.ShapeDtypeStruct((count, 2, span_len...  99.2 us
    ppermute x2, waiting for transfers between devices, scatter_sum(): received = lax.ppermute(leaving, 'tp', FAR)  24.7 us
    unnamed x38, local copies, waits for them, and re-layouts  18.1 us
    all_to_all x1, waiting for transfers between devices, local(): lax.all_to_all(regroup(prior_pieces, by_slot), 'req', split_axis=0, conca...  13.4 us
    slice x2, local copies, waits for them, and re-layouts, local(): cached[:, 1].reshape(cache_len, local_heads, HEAD_DIM)  12.7 us
    ppermute x2, waiting for transfers between devices, gather_columns(): far = lax.ppermute(share, 'tp', FAR)  12.2 us
    dot_general x1, matrix products, attend(): jnp.einsum('hqk,khd->qhd', normalized, value_rows, preferred_element_type...  12 us
    sub x1, matrix products, attend(): weights = jnp.exp(scores - highest)  10.6 us
  transfers between devices with their start and end apart: 16, of which 9 were waited for; matrix products, arithmetic and copies ran while one was open for 31% of the time, Pallas kernels for 31%

commit v1 on v0

--- a/solution.py
+++ b/solution.py
@@ -21,21 +21,25 @@
     return (center * lax.rsqrt(spread + EPSILON) * gain_row + shift_row).astype(jnp.bfloat16)
 
 
-def rotate(values, positions):
+def turns(positions, width):
     half_rot = ROTARY // 2
-    frequency = ROPE_BASE ** (-2.0 * jnp.arange(half_rot, dtype=jnp.float32) / ROTARY)
+    feature = jnp.arange(2 * HEAD_DIM, dtype=jnp.int32) % HEAD_DIM
+    rate = ROPE_BASE ** (-2.0 * (feature % half_rot).astype(jnp.float32) / ROTARY)
+    frequency = jnp.where(feature < ROTARY, rate, 0.0)
     angles = positions.astype(jnp.float32)[:, None] * frequency[None, :]
-    cosine = jnp.cos(angles)[:, None, :]
-    sine_part = jnp.sin(angles)[:, None, :]
-    first_half = values[..., :half_rot]
-    second_half = values[..., half_rot:ROTARY]
-    return jnp.concatenate(
-        [
-            first_half * cosine - second_half * sine_part,
-            second_half * cosine + first_half * sine_part,
-            values[..., ROTARY:],
-        ],
-        axis=-1,
+    cosine, sine_part = jnp.cos(angles), jnp.sin(angles)
+    first = jnp.where((feature < half_rot)[None, :], -sine_part, 0.0)
+    second = jnp.where((feature >= half_rot)[None, :], sine_part, 0.0)
+    repeats = width // (2 * HEAD_DIM)
+    return [jnp.concatenate([part] * repeats, axis=1) for part in (cosine, first, second)]
+
+
+def rotate(values, cosine, first, second):
+    half_rot = ROTARY // 2
+    return (
+        values * cosine
+        + jnp.roll(values, -half_rot, axis=1) * first
+        + jnp.roll(values, half_rot, axis=1) * second
     )
 
 
@@ -62,29 +66,44 @@
     count, span_len, _, width = pieces.shape
     half_width = width // 2
 
-    def kernel(by_slot_ref, pieces_ref, out_ref, sems):
-        copies = []
+    def kernel(by_slot_ref, pieces_ref, out_ref, held, in_sems, out_sems):
+        fetches, stores = [], []
         for device in range(count):
             for slot in range(2):
                 source = by_slot_ref[2 * (device // 2) + slot]
                 columns = pl.ds((device % 2) * half_width, half_width)
-                copies.append(
+                fetches.append(
                     pltpu.make_async_copy(
                         pieces_ref.at[source, :, :, columns],
+                        held.at[device, slot],
+                        in_sems.at[2 * device + slot],
+                    )
+                )
+                stores.append(
+                    pltpu.make_async_copy(
+                        held.at[device, slot],
                         out_ref.at[device, slot],
-                        sems.at[2 * device + slot],
-                    )
-                )
-                copies[-1].start()
-        for copy in copies:
-            copy.wait()
+                        out_sems.at[2 * device + slot],
+                    )
+                )
+                fetches[-1].start()
+        for fetch, store in zip(fetches, stores):
+            fetch.wait()
+            store.start()
+        for store in stores:
+            store.wait()
 
     return pl.pallas_call(
         kernel,
         out_shape=jax.ShapeDtypeStruct((count, 2, span_len, 2, half_width), pieces.dtype),
         in_specs=[pl.BlockSpec(memory_space=pltpu.SMEM), pl.BlockSpec(memory_space=pl.ANY)],
         out_specs=pl.BlockSpec(memory_space=pl.ANY),
-        scratch_shapes=[pltpu.SemaphoreType.DMA((2 * count,))],
+        scratch_shapes=[
+            pltpu.VMEM((count, 2, span_len, 2, half_width), pieces.dtype),
+            pltpu.SemaphoreType.DMA((2 * count,)),
+            pltpu.SemaphoreType.DMA((2 * count,)),
+        ],
+        compiler_params=pltpu.CompilerParams(vmem_limit_bytes=24 * 1024 * 1024),
         cost_estimate=pl.CostEstimate(flops=0, bytes_accessed=4 * pieces.size, transcendentals=0),
         name="regroup",
     )(by_slot, pieces)
@@ -252,28 +271,22 @@
         concat_axis=0,
         tiled=True,
     )
-    prior_received = lax.all_to_all(
-        regroup(prior_pieces, by_slot), "req", split_axis=0, concat_axis=0, tiled=True
-    )
     token_rows = gather_columns(tokens)
     inputs = token_rows.astype(jnp.float32)
     normed = layer_norm(inputs, first_gain, first_shift)
-    projected = (
-        jnp.dot(
-            normed,
-            project_weight.reshape(project_weight.shape[0], 3 * local_width),
-            preferred_element_type=jnp.float32,
-        ).reshape(stretch_len, 3, local_width)
-        + project_bias
-    )
+    projected = [
+        jnp.dot(normed, project_weight[:, part], preferred_element_type=jnp.float32)
+        + project_bias[part]
+        for part in range(3)
+    ]
     positions = prior_count + jnp.arange(stretch_len, dtype=jnp.int32)
-    queries = rotate(projected[:, 0].reshape(stretch_len, local_heads, HEAD_DIM), positions).astype(
-        jnp.bfloat16
-    )
-    new_keys = rotate(
-        projected[:, 1].reshape(stretch_len, local_heads, HEAD_DIM), positions
-    ).astype(jnp.bfloat16)
-    new_values = projected[:, 2].reshape(stretch_len, local_heads, HEAD_DIM).astype(jnp.bfloat16)
+    angle_parts = turns(positions, local_width)
+    flat_queries = rotate(projected[0], *angle_parts).astype(jnp.bfloat16)
+    flat_keys = rotate(projected[1], *angle_parts).astype(jnp.bfloat16)
+    flat_values = projected[2].astype(jnp.bfloat16)
+    queries = flat_queries.reshape(stretch_len, local_heads, HEAD_DIM)
+    new_keys = flat_keys.reshape(stretch_len, local_heads, HEAD_DIM)
+    new_values = flat_values.reshape(stretch_len, local_heads, HEAD_DIM)
     key_rows = jnp.concatenate(
         [cached[:, 0].reshape(cache_len, local_heads, HEAD_DIM), new_keys], axis=0
     )
@@ -296,10 +309,8 @@
         jnp.dot(hidden, contract_weight, preferred_element_type=jnp.float32).astype(jnp.bfloat16)
     )
     result = (residual_share.astype(jnp.float32) + down_share).astype(jnp.bfloat16)
-    fresh_cache = jnp.stack(
-        [new_keys.reshape(stretch_len, local_width), new_values.reshape(stretch_len, local_width)],
-        axis=1,
-    )
+    fresh_cache = jnp.stack([flat_keys, flat_values], axis=1)
+    fresh_cache, prior_pieces = lax.optimization_barrier((fresh_cache, prior_pieces))
     new_pieces = lax.all_to_all(
         fresh_cache.reshape(req_count, stretch_len // req_count, 2, local_width),
         "req",
@@ -307,9 +318,16 @@
         concat_axis=0,
         tiled=True,
     )
-    new_received = lax.all_to_all(
-        regroup(new_pieces, by_slot), "req", split_axis=0, concat_axis=0, tiled=True
-    )
+    prior_ordered, new_pieces = lax.optimization_barrier(
+        (regroup(prior_pieces, by_slot), new_pieces)
+    )
+    prior_received = lax.all_to_all(
+        prior_ordered, "req", split_axis=0, concat_axis=0, tiled=True
+    )
+    new_ordered, prior_received = lax.optimization_barrier(
+        (regroup(new_pieces, by_slot), prior_received)
+    )
+    new_received = lax.all_to_all(new_ordered, "req", split_axis=0, concat_axis=0, tiled=True)
     group_index = request // 2
     slots = lax.dynamic_slice_in_dim(by_slot, 2 * group_index, 2, 0)
     lengths = jnp.take(prior_len, slots)

time: 322 us -> 202 us (0.63)
  Pallas kernels: 105 us -> 13 us
  local copies, waits for them, and re-layouts: 61.4 us -> 45 us
  waiting for transfers between devices: 58 us -> 45.7 us
  other arithmetic: 26.2 us -> 31.4 us
    pallas_call x2, Pallas kernels: 99.2 us -> 7.47 us  [regroup(): pl.pallas_call(kernel, out_shape=jax.ShapeDtypeStruct((count, 2, span_len...]
    ppermute x2, waiting for transfers between devices: 12.2 us -> 1.39 us  [gather_columns(): far = lax.ppermute(share, 'tp', FAR)]
    convert_element_type x3 -> x0, local copies, waits for them, and re-layouts: 8.65 us -> none  [the longest x2 6.6 us: local(): new_keys = rotate(projected[:, 1].reshape(stretch_len, local_heads, HEAD_...]
    unnamed x38 -> x39, local copies, waits for them, and re-layouts: 18.1 us -> 11.4 us
    another operation x2 -> x1, other arithmetic: 5.93 us -> 1.06 us  [local(): fresh_cache = jnp.stack([flat_keys, flat_values], axis=1)]
    optimization_barrier x0 -> x1, local copies, waits for them, and re-layouts: none -> 3.66 us  [local(): lax.optimization_barrier((fresh_cache, prior_pieces))]
    dot_general x1, matrix products: 7.02 us -> 3.53 us  [local(): jnp.dot(second_normed, expand_weight.reshape(expand_weight.shape[0], 2 *...]
  transfers between devices with their start and end apart: 16 -> 16, of which waited for: 9 -> 7; matrix products, arithmetic and copies ran while one was open for 31% -> 54% of each run, Pallas kernels for 31% -> 4%
where the time goes in v1:
time: 202 us; the launch traced here: 201 us
  waiting for transfers between devices  45.7 us (23%)
  local copies, waits for them, and re-layouts  45 us (22%)
  matrix products  36.5 us (18%)
  other arithmetic  31.4 us (16%)
  starting transfers between devices  27.9 us (14%)
  Pallas kernels  13 us (6%)
    ppermute x2, waiting for transfers between devices, scatter_sum(): received = lax.ppermute(leaving, 'tp', FAR)  24.7 us
    all_to_all x1, waiting for transfers between devices, local(): lax.all_to_all(prior_ordered, 'req', split_axis=0, concat_axis=0, tiled=T...  16.4 us
    slice x2, local copies, waits for them, and re-layouts, local(): cached[:, 1].reshape(cache_len, local_heads, HEAD_DIM)  12.7 us
    dot_general x1, matrix products, attend(): jnp.einsum('hqk,khd->qhd', normalized, value_rows, preferred_element_type...  12 us
    unnamed x39, local copies, waits for them, and re-layouts  11.4 us
    sub x1, matrix products, attend(): weights = jnp.exp(scores - highest)  10 us
    dot_general x1, local copies, waits for them, and re-layouts, local(): jnp.dot(second_normed, expand_weight.reshape(expand_weight.shape[0], 2 *...  8.72 us
    pallas_call x2, Pallas kernels, regroup(): pl.pallas_call(kernel, out_shape=jax.ShapeDtypeStruct((count, 2, span_len...  7.47 us
  transfers between devices with their start and end apart: 16, of which 7 were waited for; matrix products, arithmetic and copies ran while one was open for 54% of the time, Pallas kernels for 4%

profile of v1, /device:TPU:0, one launch (start us, length us, event | category | flops | bytes accessed | tf_op | source)
XLA Modules:
  0.0 200.7 jit_solution(3936514656843941369)
XLA Ops:
  0.7 3.0 %collective-permute-start = (bf16[512,512]{1,0:T(8,128)(2,1)}, bf16[512,512]{1,0:T(8,128)(2,1)}, u32[]{:S(2)}, u32[]{:S(2)}) collective-permute-start(bf16[512,512]{1,0:T(8,128)(2,1)} %param.14), channel_id=1, source_target_pairs={{0,2},{2,0},{1,3},{3,1},{4,6},{6,4},{5,7},{7,5},{8,10},{10,8},{9,1... | collective-permute-start | bytes 1572872 | tf_op jit(solution)/shard_map/ppermute | solution.py:199
  3.7 5.8 %all-to-all-start = ((bf16[8,128,2,512]{3,2,1,0:T(2,128)(2,1)}), bf16[8,128,2,512]{3,2,1,0:T(2,128)(2,1)}, u32[]{:S(2)}, u32[]{:S(2)}) async-start(bf16[8,128,2,512]{3,2,1,0:T(2,128)(2,1)} %bitcast.65), calls=%async_computation | async-start | bytes 4194304 | tf_op jit(solution)/shard_map/all_to_all | solution.py:267
  10.7 6.9 %fusion.102 = (bf16[1024,1,512]{2,1,0:T(2,128)(2,1)}, bf16[1024,1,512]{2,1,0:T(2,128)(2,1)}) fusion(bf16[1024,2,512]{2,1,0:T(2,128)(2,1)} %bitcast.66), kind=kLoop, calls=%fused_computation.151 | loop fusion | bytes 4194304 | tf_op jit(solution)/shard_map/slice | solution.py:294
  20.3 5.8 %copy.25 = bf16[1024,1,512]{0,2,1:T(8,128)(2,1)} copy(bf16[1024,1,512]{2,1,0:T(2,128)(2,1)} %get-tuple-element.23) | data formatting | bytes 2097152 | tf_op jit(solution)/shard_map/slice | solution.py:291
  26.1 5.8 %copy.24 = bf16[1024,1,512]{0,2,1:T(8,128)(2,1)} copy(bf16[1024,1,512]{2,1,0:T(2,128)(2,1)} %get-tuple-element.22) | data formatting | bytes 2097152 | tf_op jit(solution)/shard_map/slice | solution.py:294
  46.5 10.0 %fusion.108 = f32[8,512]{1,0:T(8,128)S(1)} fusion(pred[512,1536]{1,0:T(8,128)(4,1)} %fusion.18, bf16[512,8,64]{0,2,1:T(8,128)(2,1)} %bitcast.77, bf16[512,8,64]{0,2,1:T(8,128)(2,1)} %bitcast.71, bf16[1024,8,64]{0,2,1:T(8,128)(2,1)} %bitcast.74), kind=kOutput, calls=%fused_computation.157 | convolution fusion | flops 833619456 | bytes 2899968 | tf_op jit(solution)/shard_map/sub | solution.py:59
  56.6 12.0 %fusion.66 = bf16[8,64,512]{2,1,0:T(8,128)(2,1)} fusion(f32[8,512]{1,0:T(8,128)S(1)} %fusion.108, bf16[512,8,64]{0,2,1:T(8,128)(2,1)} %bitcast.79, bf16[1024,8,64]{0,2,1:T(8,128)(2,1)} %bitcast.76, pred[512,1536]{1,0:T(8,128)(4,1)} %fusion.18, bf16[512,8,64]{0,2,1:T(8,128)(2,1)} %bitcast.78, bf16[512,8,64]{0,2,1:T(8,128)(2,1)} %bitcast.72, ...), kind=kOutput, calls=%fused_computation.64 | convolution fusion | flops 1648629248 | bytes 4997120 | tf_op jit(solution)/shard_map/hqk,khd->qhd/dot_general | solution.py:61
  68.6 3.1 %convolution_convert_fusion.1 = bf16[512,2048]{1,0:T(8,128)(2,1)S(1)} fusion(bf16[512,512]{0,1:T(8,128)(2,1)} %bitcast.86, bf16[512,2048]{1,0:T(8,128)(2,1)} %param.19), kind=kOutput, calls=%fused_computation.29 | convolution fusion | flops 1074790400 | bytes 4718592 | tf_op jit(solution)/shard_map/dot_general | solution.py:297
  75.7 3.7 %copy.27 = bf16[512,2,512]{2,1,0:T(2,128)(2,1)} copy(bf16[512,2,512]{0,2,1:T(8,128)(2,1)} %pad_maximum_fusion.5) | data formatting | bytes 2097152 | tf_op jit(solution)/shard_map/optimization_barrier | solution.py:313
  79.4 5.8 %all-to-all-start.1 = ((bf16[8,64,2,512]{3,2,1,0:T(2,128)(2,1)}), bf16[8,64,2,512]{3,2,1,0:T(2,128)(2,1)}, u32[]{:S(2)}, u32[]{:S(2)}) async-start(bf16[8,64,2,512]{3,2,1,0:T(2,128)(2,1)} %bitcast.69), calls=%async_computation.1 | async-start | bytes 2097152 | tf_op jit(solution)/shard_map/all_to_all | solution.py:314
  88.3 13.4 %collective-permute-done.5 = bf16[512,512]{1,0:T(8,128)(2,1)S(1)} collective-permute-done((bf16[512,512]{1,0:T(8,128)(2,1)S(1)}, bf16[512,512]{1,0:T(8,128)(2,1)S(1)}, u32[]{:S(2)}, u32[]{:S(2)}) %collective-permute-start.5) | collective-permute-done | bytes 524320 | tf_op jit(solution)/shard_map/ppermute | solution.py:230
  105.3 4.4 %regroup.2 = bf16[8,2,128,2,256]{4,3,2,1,0:T(2,128)(2,1)S(1)} custom-call(s32[8]{0:T(128)S(1)} %select_reduce_fusion.by_slot_ref, bf16[8,128,2,512]{3,2,1,0:T(2,128)(2,1)} %all-to-all-done.pieces_ref), custom_call_target="tpu_custom_call" | custom-call | bytes 4194304 | tf_op jit(solution)/shard_map/regroup/pallas_call | solution.py:96
  111.7 5.1 %all-to-all-start.2 = ((bf16[8,2,128,2,256]{4,3,2,1,0:T(2,128)(2,1)}), bf16[8,2,128,2,256]{4,3,2,1,0:T(2,128)(2,1)}, u32[]{:S(2)}, u32[]{:S(2)}) async-start(bf16[8,2,128,2,256]{4,3,2,1,0:T(2,128)(2,1)} %copy-done.1), calls=%async_computation.2 | async-start | bytes 4194304 | tf_op jit(solution)/shard_map/all_to_all | solution.py:324
  118.2 6.8 %copy.28 = bf16[256,8,2,768]{3,1,2,0:T(8,128)(2,1)} copy(bf16[256,8,2,768]{3,2,1,0:T(2,128)(2,1)} %bitcast.67) | data formatting | bytes 12582912
  125.0 8.7 %copy.26 = bf16[1536,2048]{1,0:T(8,128)(2,1)} copy(bf16[1536,2048]{0,1:T(8,128)(2,1)} %bitcast.64) | data formatting | bytes 12582912 | tf_op jit(solution)/shard_map/dot_general | solution.py:302
  137.1 3.5 %fusion.20 = f32[512,2,768]{2,0,1:T(8,128)S(1)} fusion(bf16[2,768,2048]{2,1,0:T(8,128)(2,1)S(1)} %bitcast.68, f32[2048]{0:T(1024)S(1)} %copy-done.14, f32[2048]{0:T(1024)S(1)} %copy-done.15, f32[512]{0:T(512)S(1)} %add_rsqrt_fusion, f32[512]{0:T(512)S(1)} %broadcast_multiply_fusion, bf16[512,512]{1,0:T(8,128)(2,1)S(1)} %get-tuple-element.19, ...), kind=kOutput, calls=%fused_computation.31 | convolution fusion | flops 3234856960 | bytes 11554816 | tf_op jit(solution)/shard_map/dot_general | solution.py:302
  140.6 3.1 %convolution_convert_fusion = bf16[512,2048]{1,0:T(8,128)(2,1)} fusion(bf16[768,2048]{1,0:T(8,128)(2,1)S(1)} %copy-done, f32[512,2,768]{2,0,1:T(8,128)S(1)} %fusion.20), kind=kOutput, calls=%fused_computation.28 | convolution fusion | flops 1614020608 | bytes 8388608 | tf_op jit(solution)/shard_map/dot_general | solution.py:309
  143.8 3.0 %regroup.3 = bf16[8,2,64,2,256]{4,3,2,1,0:T(2,128)(2,1)S(1)} custom-call(s32[8]{0:T(128)S(1)} %select_reduce_fusion.by_slot_ref, bf16[8,64,2,512]{3,2,1,0:T(2,128)(2,1)} %all-to-all-done.1.pieces_ref), custom_call_target="tpu_custom_call" | custom-call | bytes 2097152 | tf_op jit(solution)/shard_map/regroup/pallas_call | solution.py:96
  147.8 16.4 %all-to-all-done.2.prior_ref = bf16[8,2,128,2,256]{4,3,2,1,0:T(2,128)(2,1)} async-done(((bf16[8,2,128,2,256]{4,3,2,1,0:T(2,128)(2,1)}), bf16[8,2,128,2,256]{4,3,2,1,0:T(2,128)(2,1)}, u32[]{:S(2)}, u32[]{:S(2)}) %all-to-all-start.2) | async-done | bytes 2097184 | tf_op jit(solution)/shard_map/all_to_all | solution.py:324
  164.2 4.2 %all-to-all-start.3 = ((bf16[8,2,64,2,256]{4,3,2,1,0:T(2,128)(2,1)}), bf16[8,2,64,2,256]{4,3,2,1,0:T(2,128)(2,1)}, u32[]{:S(2)}, u32[]{:S(2)}) async-start(bf16[8,2,64,2,256]{4,3,2,1,0:T(2,128)(2,1)} %copy-done.2), calls=%async_computation.3 | async-start | bytes 2097152 | tf_op jit(solution)/shard_map/all_to_all | solution.py:330
  174.1 3.1 %select_convert_fusion = bf16[512,512]{1,0:T(8,128)(2,1)} fusion(bf16[512,512]{1,0:T(8,128)(2,1)} %collective-permute-done.9, bf16[512,512]{1,0:T(8,128)(2,1)} %collective-permute-done.10, pred[]{:T(512)S(6)} %ge.18, bf16[512,2048]{1,0:T(8,128)(2,1)} %convolution_convert_fusion, pred[]{:T(512)S(6)} %eq.27), kind=kLoop, calls=%fused_computation.80 | loop fusion | flops 2621440 | bytes 3670018 | tf_op jit(solution)/shard_map/convert_element_type | solution.py:229
  180.1 11.3 %collective-permute-done.11 = bf16[512,512]{1,0:T(8,128)(2,1)} collective-permute-done((bf16[512,512]{1,0:T(8,128)(2,1)}, bf16[512,512]{1,0:T(8,128)(2,1)}, u32[]{:S(2)}, u32[]{:S(2)}) %collective-permute-start.11) | collective-permute-done | bytes 524320 | tf_op jit(solution)/shard_map/ppermute | solution.py:230
  191.4 3.5 %add_convert_fusion = bf16[512,512]{1,0:T(8,128)(2,1)} fusion(bf16[512,512]{1,0:T(8,128)(2,1)} %collective-permute-done.11, bf16[512,512]{1,0:T(8,128)(2,1)} %add_convert_fusion.1, bf16[512,512]{1,0:T(8,128)(2,1)} %collective-permute-done.9, bf16[512,512]{1,0:T(8,128)(2,1)} %collective-permute-done.10, pred[]{:T(512)S(6)} %ge.18, ...), kind=kLoop, calls=%fused_computation.79 | loop fusion | flops 3670016 | bytes 4718594 | tf_op jit(solution)/shard_map/convert_element_type | solution.py:311
  195.0 5.5 %place_pages.1 = bf16[12,256,2,256]{3,2,1,0:T(2,128)(2,1)} custom-call(s32[2]{0:T(128)S(1)} %and_select_fusion.lengths_ref, s32[12]{0:T(128)S(1)} %reshape.168.pages_ref, bf16[8,2,128,2,256]{4,3,2,1,0:T(2,128)(2,1)} %all-to-all-done.2.prior_ref, bf16[8,2,64,2,256]{4,3,2,1,0:T(2,128)(2,1)} %all-to-all-done.3.new_ref, ...), custom_call_target="tpu_custom_call" | custom-call | bytes 6291456 | tf_op jit(solution)/shard_map/place_pages/pallas_call | solution.py:171
  (105 shorter events, 45.4 us)
Async XLA Ops:
  0.6 140.0 %copy-start = (bf16[768,2048]{1,0:T(8,128)(2,1)S(1)}, bf16[768,2048]{1,0:T(8,128)(2,1)}, u32[]{:S(2)}) copy-start(bf16[768,2048]{1,0:T(8,128)(2,1)} %param.23) | copy-start | bytes 9437188
  0.6 8.9 %copy-start.3 = (s32[8]{0:T(128)S(1)}, s32[8]{0:T(128)}, u32[]{:S(2)}) copy-start(s32[8]{0:T(128)} %param.25) | copy-start | bytes 100
  0.7 18.8 %collective-permute-start = (bf16[512,512]{1,0:T(8,128)(2,1)}, bf16[512,512]{1,0:T(8,128)(2,1)}, u32[]{:S(2)}, u32[]{:S(2)}) collective-permute-start(bf16[512,512]{1,0:T(8,128)(2,1)} %param.14), channel_id=1, source_target_pairs={{0,2},{2,0},{1,3},{3,1},{4,6},{6,4},{5,7},{7,5},{8,10},{10,8},{9,1... | collective-permute-start | bytes 1572872 | tf_op jit(solution)/shard_map/ppermute | solution.py:199
  3.7 29.7 %collective-permute-start.2 = (bf16[512,512]{1,0:T(8,128)(2,1)}, bf16[512,512]{1,0:T(8,128)(2,1)}, u32[]{:S(2)}, u32[]{:S(2)}) collective-permute-start(bf16[512,512]{1,0:T(8,128)(2,1)} %param.14), channel_id=1, source_target_pairs={{0,1},{1,0},{2,3},{3,2},{4,5},{5,4},{6,7},{7,6},{8,9},{9,8},{10,11... | collective-permute-start | bytes 1572872 | tf_op jit(solution)/shard_map/ppermute | solution.py:200
  3.7 72.0 %all-to-all-start = ((bf16[8,128,2,512]{3,2,1,0:T(2,128)(2,1)}), bf16[8,128,2,512]{3,2,1,0:T(2,128)(2,1)}, u32[]{:S(2)}, u32[]{:S(2)}) async-start(bf16[8,128,2,512]{3,2,1,0:T(2,128)(2,1)} %bitcast.65), calls=%async_computation | async-start | bytes 4194304 | tf_op jit(solution)/shard_map/all_to_all | solution.py:267
  10.7 6.9 %copy-start.13 = (f32[3,512]{1,0:T(4,128)S(1)}, f32[3,512]{1,0:T(4,128)}, u32[]{:S(2)}) copy-start(f32[3,512]{1,0:T(4,128)} %param.18) | copy-start | bytes 18436
  19.5 13.9 %collective-permute-start.1 = (bf16[512,512]{1,0:T(8,128)(2,1)}, bf16[512,512]{1,0:T(8,128)(2,1)}, u32[]{:S(2)}, u32[]{:S(2)}) collective-permute-start(bf16[512,512]{1,0:T(8,128)(2,1)} %collective-permute-done), channel_id=1, source_target_pairs={{0,1},{1,0},{2,3},{3,2},{4,5},{5,4},{6,7},{7,6},{8,9},{9,8},{10,11... | collective-permute-start | bytes 1572872 | tf_op jit(solution)/shard_map/ppermute | solution.py:201
  32.0 5.8 %slice-start = ((s8[6291456]{0:T(1024)(128)(4,1)}), s8[4194304]{0:T(1024)(128)(4,1)S(1)}, s32[]{:S(2)}) async-start(s8[6291456]{0:T(1024)(128)(4,1)} %bitcast.84), calls=%async_computation.4 | async-start | bytes 8388608
  68.6 6.1 %copy-start.9 = (bf16[512,512]{0,1:T(8,128)(2,1)S(1)}, bf16[512,512]{0,1:T(8,128)(2,1)}, u32[]{:S(2)}) copy-start(bf16[512,512]{0,1:T(8,128)(2,1)} %fusion.74) | copy-start | bytes 1572868
  68.6 6.1 %copy-start.10 = (bf16[512,512]{0,1:T(8,128)(2,1)S(1)}, bf16[512,512]{0,1:T(8,128)(2,1)}, u32[]{:S(2)}) copy-start(bf16[512,512]{0,1:T(8,128)(2,1)} %fusion.63) | copy-start | bytes 1572868
  74.1 11.0 %collective-permute-start.3 = (bf16[512,512]{1,0:T(8,128)(2,1)}, bf16[512,512]{1,0:T(8,128)(2,1)}, u32[]{:S(2)}, u32[]{:S(2)}) collective-permute-start(bf16[512,512]{1,0:T(8,128)(2,1)} %get-tuple-element.21), channel_id=1, source_target_pairs={{0,1},{1,0},{2,3},{3,2},{4,5},{5,4},{6,7},{7,6},{8,9},{9,8},{10,11... | collective-permute-start | bytes 1572872 | tf_op jit(solution)/shard_map/ppermute | solution.py:222
  74.4 10.7 %collective-permute-start.4 = (bf16[512,512]{1,0:T(8,128)(2,1)}, bf16[512,512]{1,0:T(8,128)(2,1)}, u32[]{:S(2)}, u32[]{:S(2)}) collective-permute-start(bf16[512,512]{1,0:T(8,128)(2,1)} %get-tuple-element.20), channel_id=1, source_target_pairs={{0,1},{1,0},{2,3},{3,2},{4,5},{5,4},{6,7},{7,6},{8,9},{9,8},{10,11... | collective-permute-start | bytes 1572872 | tf_op jit(solution)/shard_map/ppermute | solution.py:222
  79.4 32.3 %all-to-all-start.1 = ((bf16[8,64,2,512]{3,2,1,0:T(2,128)(2,1)}), bf16[8,64,2,512]{3,2,1,0:T(2,128)(2,1)}, u32[]{:S(2)}, u32[]{:S(2)}) async-start(bf16[8,64,2,512]{3,2,1,0:T(2,128)(2,1)} %bitcast.69), calls=%async_computation.1 | async-start | bytes 2097152 | tf_op jit(solution)/shard_map/all_to_all | solution.py:314
  85.2 16.6 %copy-start.5 = (bf16[512,2048]{1,0:T(8,128)(2,1)S(1)}, bf16[512,2048]{1,0:T(8,128)(2,1)}, u32[]{:S(2)}) copy-start(bf16[512,2048]{1,0:T(8,128)(2,1)} %copy-done.4) | copy-start | bytes 6291460
  85.2 20.0 %copy-start.16 = (s32[8]{0:T(128)S(1)}, s32[8]{0:T(128)}, u32[]{:S(2)}) copy-start(s32[8]{0:T(128)} %param.26) | copy-start | bytes 100
  87.6 14.1 %collective-permute-start.5 = (bf16[512,512]{1,0:T(8,128)(2,1)S(1)}, bf16[512,512]{1,0:T(8,128)(2,1)S(1)}, u32[]{:S(2)}, u32[]{:S(2)}) collective-permute-start(bf16[512,512]{1,0:T(8,128)(2,1)S(1)} %select_convert_fusion.1), channel_id=1, source_target_pairs={{0,2},{2,0},{1,3},{3,1},{4,6},{6,4},{5,7},{7,5},{8,10},{10,8},{9,1... | collective-permute-start | bytes 1572872 | tf_op jit(solution)/shard_map/ppermute | solution.py:230
  104.5 13.7 %collective-permute-start.6 = (bf16[512,512]{1,0:T(8,128)(2,1)}, bf16[512,512]{1,0:T(8,128)(2,1)}, u32[]{:S(2)}, u32[]{:S(2)}) collective-permute-start(bf16[512,512]{1,0:T(8,128)(2,1)} %add_convert_fusion.1), channel_id=1, source_target_pairs={{0,2},{2,0},{1,3},{3,1},{4,6},{6,4},{5,7},{7,5},{8,10},{10,8},{9,1... | collective-permute-start | bytes 1572872 | tf_op jit(solution)/shard_map/ppermute | solution.py:199
  111.7 52.5 %all-to-all-start.2 = ((bf16[8,2,128,2,256]{4,3,2,1,0:T(2,128)(2,1)}), bf16[8,2,128,2,256]{4,3,2,1,0:T(2,128)(2,1)}, u32[]{:S(2)}, u32[]{:S(2)}) async-start(bf16[8,2,128,2,256]{4,3,2,1,0:T(2,128)(2,1)} %copy-done.1), calls=%async_computation.2 | async-start | bytes 4194304 | tf_op jit(solution)/shard_map/all_to_all | solution.py:324
  116.8 16.9 %collective-permute-start.8 = (bf16[512,512]{1,0:T(8,128)(2,1)}, bf16[512,512]{1,0:T(8,128)(2,1)}, u32[]{:S(2)}, u32[]{:S(2)}) collective-permute-start(bf16[512,512]{1,0:T(8,128)(2,1)} %add_convert_fusion.1), channel_id=1, source_target_pairs={{0,1},{1,0},{2,3},{3,2},{4,5},{5,4},{6,7},{7,6},{8,9},{9,8},{10,11... | collective-permute-start | bytes 1572872 | tf_op jit(solution)/shard_map/ppermute | solution.py:200
  118.2 15.5 %collective-permute-start.7 = (bf16[512,512]{1,0:T(8,128)(2,1)}, bf16[512,512]{1,0:T(8,128)(2,1)}, u32[]{:S(2)}, u32[]{:S(2)}) collective-permute-start(bf16[512,512]{1,0:T(8,128)(2,1)} %collective-permute-done.6), channel_id=1, source_target_pairs={{0,1},{1,0},{2,3},{3,2},{4,5},{5,4},{6,7},{7,6},{8,9},{9,8},{10,11... | collective-permute-start | bytes 1572872 | tf_op jit(solution)/shard_map/ppermute | solution.py:201
  164.2 30.7 %all-to-all-start.3 = ((bf16[8,2,64,2,256]{4,3,2,1,0:T(2,128)(2,1)}), bf16[8,2,64,2,256]{4,3,2,1,0:T(2,128)(2,1)}, u32[]{:S(2)}, u32[]{:S(2)}) async-start(bf16[8,2,64,2,256]{4,3,2,1,0:T(2,128)(2,1)} %copy-done.2), calls=%async_computation.3 | async-start | bytes 2097152 | tf_op jit(solution)/shard_map/all_to_all | solution.py:330
  171.1 2.3 %collective-permute-start.9 = (bf16[512,512]{1,0:T(8,128)(2,1)}, bf16[512,512]{1,0:T(8,128)(2,1)}, u32[]{:S(2)}, u32[]{:S(2)}) collective-permute-start(bf16[512,512]{1,0:T(8,128)(2,1)} %get-tuple-element.15), channel_id=1, source_target_pairs={{0,1},{1,0},{2,3},{3,2},{4,5},{5,4},{6,7},{7,6},{8,9},{9,8},{10,11... | collective-permute-start | bytes 1572872 | tf_op jit(solution)/shard_map/ppermute | solution.py:222
  171.1 3.0 %collective-permute-start.10 = (bf16[512,512]{1,0:T(8,128)(2,1)}, bf16[512,512]{1,0:T(8,128)(2,1)}, u32[]{:S(2)}, u32[]{:S(2)}) collective-permute-start(bf16[512,512]{1,0:T(8,128)(2,1)} %get-tuple-element.14), channel_id=1, source_target_pairs={{0,1},{1,0},{2,3},{3,2},{4,5},{5,4},{6,7},{7,6},{8,9},{9,8},{10,11... | collective-permute-start | bytes 1572872 | tf_op jit(solution)/shard_map/ppermute | solution.py:222
  177.1 14.3 %collective-permute-start.11 = (bf16[512,512]{1,0:T(8,128)(2,1)}, bf16[512,512]{1,0:T(8,128)(2,1)}, u32[]{:S(2)}, u32[]{:S(2)}) collective-permute-start(bf16[512,512]{1,0:T(8,128)(2,1)} %select_convert_fusion), channel_id=1, source_target_pairs={{0,2},{2,0},{1,3},{3,1},{4,6},{6,4},{5,7},{7,5},{8,10},{10,8},{9,1... | collective-permute-start | bytes 1572872 | tf_op jit(solution)/shard_map/ppermute | solution.py:230
  (11 other events, 24.6 us)

commit v2 on v1

--- a/solution.py
+++ b/solution.py
@@ -212,7 +212,7 @@
     )
 
 
-def scatter_sum(partial):
+def scatter_sum(partial, earlier):
     me = lax.axis_index("tp")
     odd, high = me % 2 == 1, me >= 2
     width = partial.shape[1] // 4
@@ -227,8 +227,9 @@
     low_half = near_sum(blocks[0], blocks[1])
     high_half = near_sum(blocks[2], blocks[3])
     leaving = jnp.where(high, low_half, high_half).astype(jnp.bfloat16)
+    leaving, earlier = lax.optimization_barrier((leaving, earlier))
     received = lax.ppermute(leaving, "tp", FAR)
-    return jnp.where(high, high_half, low_half) + received.astype(jnp.float32)
+    return jnp.where(high, high_half, low_half) + received.astype(jnp.float32), earlier
 
 
 def local(
@@ -287,28 +288,6 @@
     queries = flat_queries.reshape(stretch_len, local_heads, HEAD_DIM)
     new_keys = flat_keys.reshape(stretch_len, local_heads, HEAD_DIM)
     new_values = flat_values.reshape(stretch_len, local_heads, HEAD_DIM)
-    key_rows = jnp.concatenate(
-        [cached[:, 0].reshape(cache_len, local_heads, HEAD_DIM), new_keys], axis=0
-    )
-    value_rows = jnp.concatenate(
-        [cached[:, 1].reshape(cache_len, local_heads, HEAD_DIM), new_values], axis=0
-    )
-    mixture = attend(queries, key_rows, value_rows, prior_count).reshape(stretch_len, local_width)
-    partial_value = jnp.dot(mixture, output_weight, preferred_element_type=jnp.float32)
-    mixer_share = scatter_sum(partial_value.astype(jnp.bfloat16))
-    residual_share = (tokens.astype(jnp.float32) + mixer_share).astype(jnp.bfloat16)
-    residual = gather_columns(residual_share)
-    second_normed = layer_norm(residual.astype(jnp.float32), second_gain, second_shift)
-    gate_up = jnp.dot(
-        second_normed,
-        expand_weight.reshape(expand_weight.shape[0], 2 * local_hidden),
-        preferred_element_type=jnp.float32,
-    ).reshape(stretch_len, 2, local_hidden)
-    hidden = (jax.nn.silu(gate_up[:, 0]) * gate_up[:, 1]).astype(jnp.bfloat16)
-    down_share = scatter_sum(
-        jnp.dot(hidden, contract_weight, preferred_element_type=jnp.float32).astype(jnp.bfloat16)
-    )
-    result = (residual_share.astype(jnp.float32) + down_share).astype(jnp.bfloat16)
     fresh_cache = jnp.stack([flat_keys, flat_values], axis=1)
     fresh_cache, prior_pieces = lax.optimization_barrier((fresh_cache, prior_pieces))
     new_pieces = lax.all_to_all(
@@ -318,16 +297,40 @@
         concat_axis=0,
         tiled=True,
     )
+    key_rows = jnp.concatenate(
+        [cached[:, 0].reshape(cache_len, local_heads, HEAD_DIM), new_keys], axis=0
+    )
+    value_rows = jnp.concatenate(
+        [cached[:, 1].reshape(cache_len, local_heads, HEAD_DIM), new_values], axis=0
+    )
+    mixture = attend(queries, key_rows, value_rows, prior_count).reshape(stretch_len, local_width)
+    partial_value = jnp.dot(mixture, output_weight, preferred_element_type=jnp.float32)
+    mixer_share, new_pieces = scatter_sum(partial_value.astype(jnp.bfloat16), new_pieces)
     prior_ordered, new_pieces = lax.optimization_barrier(
         (regroup(prior_pieces, by_slot), new_pieces)
     )
     prior_received = lax.all_to_all(
         prior_ordered, "req", split_axis=0, concat_axis=0, tiled=True
     )
+    residual_share = (tokens.astype(jnp.float32) + mixer_share).astype(jnp.bfloat16)
+    residual = gather_columns(residual_share)
+    second_normed = layer_norm(residual.astype(jnp.float32), second_gain, second_shift)
+    second_normed, prior_received = lax.optimization_barrier((second_normed, prior_received))
+    gate_up = jnp.dot(
+        second_normed,
+        expand_weight.reshape(expand_weight.shape[0], 2 * local_hidden),
+        preferred_element_type=jnp.float32,
+    ).reshape(stretch_len, 2, local_hidden)
+    hidden = (jax.nn.silu(gate_up[:, 0]) * gate_up[:, 1]).astype(jnp.bfloat16)
     new_ordered, prior_received = lax.optimization_barrier(
         (regroup(new_pieces, by_slot), prior_received)
     )
     new_received = lax.all_to_all(new_ordered, "req", split_axis=0, concat_axis=0, tiled=True)
+    down_share, prior_received = scatter_sum(
+        jnp.dot(hidden, contract_weight, preferred_element_type=jnp.float32).astype(jnp.bfloat16),
+        prior_received,
+    )
+    result = (residual_share.astype(jnp.float32) + down_share).astype(jnp.bfloat16)
     group_index = request // 2
     slots = lax.dynamic_slice_in_dim(by_slot, 2 * group_index, 2, 0)
     lengths = jnp.take(prior_len, slots)

time: 202 us -> 203 us (level)
  waiting for transfers between devices: 45.7 us -> 48.5 us
    all_to_all x1, waiting for transfers between devices: 0.01 us -> 12.4 us  [local(): lax.all_to_all(cached.reshape(req_count, cache_len // req_count, 2, local...]
    ppermute x2, waiting for transfers between devices: 1.39 us -> 12.9 us  [gather_columns(): far = lax.ppermute(share, 'tp', FAR)]
    ppermute x2, waiting for transfers between devices: 24.7 us -> 13.3 us  [scatter_sum(): received = lax.ppermute(leaving, 'tp', FAR)]
    all_to_all x1, waiting for transfers between devices: 16.4 us -> 5.18 us  [local(): lax.all_to_all(prior_ordered, 'req', split_axis=0, concat_axis=0, tiled=T...]
    dot_general x1, matrix products: 3.53 us -> 6.26 us  [local(): jnp.dot(second_normed, expand_weight.reshape(expand_weight.shape[0], 2 *...]
    select_n x2, other arithmetic: 3.7 us -> 1.22 us  [near_sum(): received = lax.ppermute(jnp.where(odd, even_block, odd_block), 'tp', NEAR)]
    ppermute x4, waiting for transfers between devices: 2.5 us -> 4.64 us  [near_sum(): received = lax.ppermute(jnp.where(odd, even_block, odd_block), 'tp', NEAR)]
    convert_element_type x1 -> x2, other arithmetic: 1.18 us -> 3.31 us  [layer_norm(): (center * lax.rsqrt(spread + EPSILON) * gain_row + shift_row).astype(jnp....]
  transfers between devices with their start and end apart: 16 -> 16, of which waited for: 7 -> 9; matrix products, arithmetic and copies ran while one was open for 54% -> 51% of each run, Pallas kernels for 4% -> 4%
where the time goes in v2:
time: 203 us; the launch traced here: 202 us
  waiting for transfers between devices  48.5 us (24%)
  local copies, waits for them, and re-layouts  44.6 us (22%)
  matrix products  37.1 us (18%)
  other arithmetic  30 us (15%)
  starting transfers between devices  27.1 us (13%)
  Pallas kernels  13 us (6%)
    ppermute x2, waiting for transfers between devices, scatter_sum(): received = lax.ppermute(leaving, 'tp', FAR)  13.3 us
    ppermute x2, waiting for transfers between devices, gather_columns(): far = lax.ppermute(share, 'tp', FAR)  12.9 us
    slice x2, local copies, waits for them, and re-layouts, local(): cached[:, 1].reshape(cache_len, local_heads, HEAD_DIM)  12.7 us
    all_to_all x1, waiting for transfers between devices, local(): lax.all_to_all(cached.reshape(req_count, cache_len // req_count, 2, local...  12.4 us
    dot_general x1, matrix products, attend(): jnp.einsum('hqk,khd->qhd', normalized, value_rows, preferred_element_type...  12 us
    unnamed x41, local copies, waits for them, and re-layouts  11 us
    sub x1, matrix products, attend(): weights = jnp.exp(scores - highest)  10.1 us
    dot_general x1, local copies, waits for them, and re-layouts, local(): jnp.dot(second_normed, expand_weight.reshape(expand_weight.shape[0], 2 *...  8.7 us
  transfers between devices with their start and end apart: 16, of which 9 were waited for; matrix products, arithmetic and copies ran while one was open for 51% of the time, Pallas kernels for 4%

profile of v2, /device:TPU:0, one launch (start us, length us, event | category | flops | bytes accessed | tf_op | source)
XLA Modules:
  0.0 201.6 jit_solution(11616903463790663890)
XLA Ops:
  0.7 3.0 %collective-permute-start = (bf16[512,512]{1,0:T(8,128)(2,1)}, bf16[512,512]{1,0:T(8,128)(2,1)}, u32[]{:S(2)}, u32[]{:S(2)}) collective-permute-start(bf16[512,512]{1,0:T(8,128)(2,1)} %param.14), channel_id=1, source_target_pairs={{0,2},{2,0},{1,3},{3,1},{4,6},{6,4},{5,7},{7,5},{8,10},{10,8},{9,1... | collective-permute-start | bytes 1572872 | tf_op jit(solution)/shard_map/ppermute | solution.py:199
  3.7 5.8 %all-to-all-start = ((bf16[8,128,2,512]{3,2,1,0:T(2,128)(2,1)}), bf16[8,128,2,512]{3,2,1,0:T(2,128)(2,1)}, u32[]{:S(2)}, u32[]{:S(2)}) async-start(bf16[8,128,2,512]{3,2,1,0:T(2,128)(2,1)} %bitcast.65), calls=%async_computation | async-start | bytes 4194304 | tf_op jit(solution)/shard_map/all_to_all | solution.py:268
  10.7 6.9 %fusion.97 = (bf16[1024,1,512]{2,1,0:T(2,128)(2,1)}, bf16[1024,1,512]{2,1,0:T(2,128)(2,1)}) fusion(bf16[1024,2,512]{2,1,0:T(2,128)(2,1)} %bitcast.66), kind=kLoop, calls=%fused_computation.147 | loop fusion | bytes 4194304 | tf_op jit(solution)/shard_map/slice | solution.py:304
  20.2 5.8 %copy.25 = bf16[1024,1,512]{0,2,1:T(8,128)(2,1)} copy(bf16[1024,1,512]{2,1,0:T(2,128)(2,1)} %get-tuple-element.35) | data formatting | bytes 2097152 | tf_op jit(solution)/shard_map/slice | solution.py:301
  26.1 5.8 %copy.24 = bf16[1024,1,512]{0,2,1:T(8,128)(2,1)} copy(bf16[1024,1,512]{2,1,0:T(2,128)(2,1)} %get-tuple-element.34) | data formatting | bytes 2097152 | tf_op jit(solution)/shard_map/slice | solution.py:304
  46.1 12.4 %all-to-all-done.pieces_ref = bf16[8,128,2,512]{3,2,1,0:T(2,128)(2,1)} async-done(((bf16[8,128,2,512]{3,2,1,0:T(2,128)(2,1)}), bf16[8,128,2,512]{3,2,1,0:T(2,128)(2,1)}, u32[]{:S(2)}, u32[]{:S(2)}) %all-to-all-start) | async-done | bytes 2097184 | tf_op jit(solution)/shard_map/all_to_all | solution.py:268
  58.5 3.6 %copy.26 = bf16[512,2,512]{2,1,0:T(2,128)(2,1)} copy(bf16[512,2,512]{0,2,1:T(8,128)(2,1)} %pad_maximum_fusion.5) | data formatting | bytes 2097152 | tf_op jit(solution)/shard_map/optimization_barrier | solution.py:292
  62.2 4.4 %all-to-all-start.1 = ((bf16[8,64,2,512]{3,2,1,0:T(2,128)(2,1)}), bf16[8,64,2,512]{3,2,1,0:T(2,128)(2,1)}, u32[]{:S(2)}, u32[]{:S(2)}) async-start(bf16[8,64,2,512]{3,2,1,0:T(2,128)(2,1)} %bitcast.69), calls=%async_computation.1 | async-start | bytes 2097152 | tf_op jit(solution)/shard_map/all_to_all | solution.py:293
  66.6 10.1 %fusion.103 = f32[8,512]{1,0:T(8,128)S(1)} fusion(pred[512,1536]{1,0:T(8,128)(4,1)} %fusion.18, bf16[512,8,64]{0,2,1:T(8,128)(2,1)} %bitcast.77, bf16[512,8,64]{0,2,1:T(8,128)(2,1)} %bitcast.72, bf16[1024,8,64]{0,2,1:T(8,128)(2,1)} %bitcast.74), kind=kOutput, calls=%fused_computation.153 | convolution fusion | flops 833619456 | bytes 2899968 | tf_op jit(solution)/shard_map/sub | solution.py:59
  76.7 12.0 %fusion.61 = bf16[8,64,512]{2,1,0:T(8,128)(2,1)} fusion(f32[8,512]{1,0:T(8,128)S(1)} %fusion.103, bf16[512,8,64]{0,2,1:T(8,128)(2,1)} %bitcast.80, bf16[1024,8,64]{0,2,1:T(8,128)(2,1)} %bitcast.76, pred[512,1536]{1,0:T(8,128)(4,1)} %fusion.18, bf16[512,8,64]{0,2,1:T(8,128)(2,1)} %bitcast.78, bf16[512,8,64]{0,2,1:T(8,128)(2,1)} %bitcast.73, ...), kind=kOutput, calls=%fused_computation.60 | convolution fusion | flops 1648629248 | bytes 4997120 | tf_op jit(solution)/shard_map/hqk,khd->qhd/dot_general | solution.py:61
  88.7 3.0 %convolution_convert_fusion.1 = bf16[512,2048]{1,0:T(8,128)(2,1)S(1)} fusion(bf16[512,512]{0,1:T(8,128)(2,1)} %bitcast.86, bf16[512,2048]{1,0:T(8,128)(2,1)} %param.19), kind=kOutput, calls=%fused_computation.29 | convolution fusion | flops 1074790400 | bytes 4718592 | tf_op jit(solution)/shard_map/dot_general | solution.py:307
  97.3 4.4 %regroup.2 = bf16[8,2,128,2,256]{4,3,2,1,0:T(2,128)(2,1)S(1)} custom-call(s32[8]{0:T(128)S(1)} %select_reduce_fusion.by_slot_ref, bf16[8,128,2,512]{3,2,1,0:T(2,128)(2,1)} %all-to-all-done.pieces_ref), custom_call_target="tpu_custom_call" | custom-call | bytes 4194304 | tf_op jit(solution)/shard_map/regroup/pallas_call | solution.py:96
  103.0 5.7 %all-to-all-start.2 = ((bf16[8,2,128,2,256]{4,3,2,1,0:T(2,128)(2,1)}), bf16[8,2,128,2,256]{4,3,2,1,0:T(2,128)(2,1)}, u32[]{:S(2)}, u32[]{:S(2)}) async-start(bf16[8,2,128,2,256]{4,3,2,1,0:T(2,128)(2,1)} %copy-done.1), calls=%async_computation.2 | async-start | bytes 4194304 | tf_op jit(solution)/shard_map/all_to_all | solution.py:312
  110.9 3.5 %add_convert_fusion.1 = bf16[512,512]{1,0:T(8,128)(2,1)} fusion(bf16[512,512]{1,0:T(8,128)(2,1)} %collective-permute-done.5, bf16[512,512]{1,0:T(8,128)(2,1)} %param.14, bf16[512,512]{1,0:T(8,128)(2,1)} %copy-done.9, bf16[512,512]{1,0:T(8,128)(2,1)} %copy-done.10, pred[]{:T(512)S(6)} %ge.18, bf16[512,2048]{1,0:T(8,128)(2,1)} %copy-done.5, pred[]{:T(512)S(6)} %eq.27), kind=kLoop, calls=%fused_computation.79 | loop fusion | flops 3670016 | bytes 4718594 | tf_op jit(solution)/shard_map/convert_element_type | solution.py:315
  114.9 12.9 %collective-permute-done.6 = bf16[512,512]{1,0:T(8,128)(2,1)} collective-permute-done((bf16[512,512]{1,0:T(8,128)(2,1)}, bf16[512,512]{1,0:T(8,128)(2,1)}, u32[]{:S(2)}, u32[]{:S(2)}) %collective-permute-start.6) | collective-permute-done | bytes 524320 | tf_op jit(solution)/shard_map/ppermute | solution.py:199
  127.9 6.8 %copy.28 = bf16[256,8,2,768]{3,1,2,0:T(8,128)(2,1)} copy(bf16[256,8,2,768]{3,2,1,0:T(2,128)(2,1)} %bitcast.67) | data formatting | bytes 12582912
  134.6 8.7 %copy.27 = bf16[1536,2048]{1,0:T(8,128)(2,1)} copy(bf16[1536,2048]{0,1:T(8,128)(2,1)} %bitcast.64) | data formatting | bytes 12582912 | tf_op jit(solution)/shard_map/dot_general | solution.py:319
  151.9 5.2 %all-to-all-done.2.prior_ref = bf16[8,2,128,2,256]{4,3,2,1,0:T(2,128)(2,1)} async-done(((bf16[8,2,128,2,256]{4,3,2,1,0:T(2,128)(2,1)}), bf16[8,2,128,2,256]{4,3,2,1,0:T(2,128)(2,1)}, u32[]{:S(2)}, u32[]{:S(2)}) %all-to-all-start.2) | async-done | bytes 2097184 | tf_op jit(solution)/shard_map/all_to_all | solution.py:312
  157.1 4.2 %all-to-all-start.3 = ((bf16[8,2,64,2,256]{4,3,2,1,0:T(2,128)(2,1)}), bf16[8,2,64,2,256]{4,3,2,1,0:T(2,128)(2,1)}, u32[]{:S(2)}, u32[]{:S(2)}) async-start(bf16[8,2,64,2,256]{4,3,2,1,0:T(2,128)(2,1)} %copy-done.2), calls=%async_computation.3 | async-start | bytes 2097152 | tf_op jit(solution)/shard_map/all_to_all | solution.py:328
  161.4 6.3 %fusion.19 = f32[512,2,768]{2,0,1:T(8,128)S(1)} fusion(bf16[2,768,2048]{2,1,0:T(8,128)(2,1)} %bitcast.68, bf16[512,2048]{1,0:T(8,128)(2,1)} %fusion.13), kind=kOutput, calls=%fused_computation.32 | convolution fusion | flops 3221225472 | bytes 11534336 | tf_op jit(solution)/shard_map/dot_general | solution.py:319
  174.9 3.1 %select_convert_fusion = bf16[512,512]{1,0:T(8,128)(2,1)} fusion(bf16[512,512]{1,0:T(8,128)(2,1)} %collective-permute-done.9, bf16[512,512]{1,0:T(8,128)(2,1)} %collective-permute-done.10, pred[]{:T(512)S(6)} %ge.18, bf16[512,2048]{1,0:T(8,128)(2,1)} %copy-done.4, pred[]{:T(512)S(6)} %eq.27), kind=kLoop, calls=%fused_computation.76 | loop fusion | flops 2621440 | bytes 3670018 | tf_op jit(solution)/shard_map/convert_element_type | solution.py:229
  181.1 11.2 %collective-permute-done.11 = bf16[512,512]{1,0:T(8,128)(2,1)} collective-permute-done((bf16[512,512]{1,0:T(8,128)(2,1)}, bf16[512,512]{1,0:T(8,128)(2,1)}, u32[]{:S(2)}, u32[]{:S(2)}) %collective-permute-start.11) | collective-permute-done | bytes 524320 | tf_op jit(solution)/shard_map/ppermute | solution.py:231
  192.3 3.5 %add_convert_fusion = bf16[512,512]{1,0:T(8,128)(2,1)} fusion(bf16[512,512]{1,0:T(8,128)(2,1)} %collective-permute-done.11, bf16[512,512]{1,0:T(8,128)(2,1)} %add_convert_fusion.1, bf16[512,512]{1,0:T(8,128)(2,1)} %collective-permute-done.9, bf16[512,512]{1,0:T(8,128)(2,1)} %collective-permute-done.10, pred[]{:T(512)S(6)} %ge.18, ...), kind=kLoop, calls=%fused_computation.75 | loop fusion | flops 3670016 | bytes 4718594 | tf_op jit(solution)/shard_map/convert_element_type | solution.py:333
  195.9 5.5 %place_pages.1 = bf16[12,256,2,256]{3,2,1,0:T(2,128)(2,1)} custom-call(s32[2]{0:T(128)S(1)} %and_select_fusion.lengths_ref, s32[12]{0:T(128)S(1)} %reshape.169.pages_ref, bf16[8,2,128,2,256]{4,3,2,1,0:T(2,128)(2,1)} %all-to-all-done.2.prior_ref, bf16[8,2,64,2,256]{4,3,2,1,0:T(2,128)(2,1)} %all-to-all-done.3.new_ref, ...), custom_call_target="tpu_custom_call" | custom-call | bytes 6291456 | tf_op jit(solution)/shard_map/place_pages/pallas_call | solution.py:171
  (108 shorter events, 46.3 us)
Async XLA Ops:
  0.6 167.0 %copy-start = (bf16[768,2048]{1,0:T(8,128)(2,1)S(1)}, bf16[768,2048]{1,0:T(8,128)(2,1)}, u32[]{:S(2)}) copy-start(bf16[768,2048]{1,0:T(8,128)(2,1)} %param.23) | copy-start | bytes 9437188
  0.6 8.9 %copy-start.3 = (s32[8]{0:T(128)S(1)}, s32[8]{0:T(128)}, u32[]{:S(2)}) copy-start(s32[8]{0:T(128)} %param.25) | copy-start | bytes 100
  0.7 18.8 %collective-permute-start = (bf16[512,512]{1,0:T(8,128)(2,1)}, bf16[512,512]{1,0:T(8,128)(2,1)}, u32[]{:S(2)}, u32[]{:S(2)}) collective-permute-start(bf16[512,512]{1,0:T(8,128)(2,1)} %param.14), channel_id=1, source_target_pairs={{0,2},{2,0},{1,3},{3,1},{4,6},{6,4},{5,7},{7,5},{8,10},{10,8},{9,1... | collective-permute-start | bytes 1572872 | tf_op jit(solution)/shard_map/ppermute | solution.py:199
  3.7 29.7 %collective-permute-start.2 = (bf16[512,512]{1,0:T(8,128)(2,1)}, bf16[512,512]{1,0:T(8,128)(2,1)}, u32[]{:S(2)}, u32[]{:S(2)}) collective-permute-start(bf16[512,512]{1,0:T(8,128)(2,1)} %param.14), channel_id=1, source_target_pairs={{0,1},{1,0},{2,3},{3,2},{4,5},{5,4},{6,7},{7,6},{8,9},{9,8},{10,11... | collective-permute-start | bytes 1572872 | tf_op jit(solution)/shard_map/ppermute | solution.py:200
  3.7 54.8 %all-to-all-start = ((bf16[8,128,2,512]{3,2,1,0:T(2,128)(2,1)}), bf16[8,128,2,512]{3,2,1,0:T(2,128)(2,1)}, u32[]{:S(2)}, u32[]{:S(2)}) async-start(bf16[8,128,2,512]{3,2,1,0:T(2,128)(2,1)} %bitcast.65), calls=%async_computation | async-start | bytes 4194304 | tf_op jit(solution)/shard_map/all_to_all | solution.py:268
  10.6 6.9 %copy-start.16 = (f32[3,512]{1,0:T(4,128)S(1)}, f32[3,512]{1,0:T(4,128)}, u32[]{:S(2)}) copy-start(f32[3,512]{1,0:T(4,128)} %param.18) | copy-start | bytes 18436
  19.4 13.9 %collective-permute-start.1 = (bf16[512,512]{1,0:T(8,128)(2,1)}, bf16[512,512]{1,0:T(8,128)(2,1)}, u32[]{:S(2)}, u32[]{:S(2)}) collective-permute-start(bf16[512,512]{1,0:T(8,128)(2,1)} %collective-permute-done), channel_id=1, source_target_pairs={{0,1},{1,0},{2,3},{3,2},{4,5},{5,4},{6,7},{7,6},{8,9},{9,8},{10,11... | collective-permute-start | bytes 1572872 | tf_op jit(solution)/shard_map/ppermute | solution.py:201
  31.9 5.8 %slice-start = ((s8[6291456]{0:T(1024)(128)(4,1)}), s8[4194304]{0:T(1024)(128)(4,1)S(1)}, s32[]{:S(2)}) async-start(s8[6291456]{0:T(1024)(128)(4,1)} %bitcast.84), calls=%async_computation.4 | async-start | bytes 8388608
  35.2 2.5 %slice-start.1 = ((s8[6291456]{0:T(1024)(128)(4,1)}), s8[2097152]{0:T(1024)(128)(4,1)S(1)}, s32[]{:S(2)}) async-start(s8[6291456]{0:T(1024)(128)(4,1)} %bitcast.84), calls=%async_computation.5 | async-start | bytes 4194304
  62.2 34.5 %all-to-all-start.1 = ((bf16[8,64,2,512]{3,2,1,0:T(2,128)(2,1)}), bf16[8,64,2,512]{3,2,1,0:T(2,128)(2,1)}, u32[]{:S(2)}, u32[]{:S(2)}) async-start(bf16[8,64,2,512]{3,2,1,0:T(2,128)(2,1)} %bitcast.69), calls=%async_computation.1 | async-start | bytes 2097152 | tf_op jit(solution)/shard_map/all_to_all | solution.py:293
  91.7 2.9 %copy-start.5 = (bf16[512,2048]{1,0:T(8,128)(2,1)}, bf16[512,2048]{1,0:T(8,128)(2,1)S(1)}, u32[]{:S(2)}) copy-start(bf16[512,2048]{1,0:T(8,128)(2,1)S(1)} %convolution_convert_fusion.1) | copy-start | bytes 6291460
  91.7 5.4 %copy-start.17 = (s32[8]{0:T(128)S(1)}, s32[8]{0:T(128)}, u32[]{:S(2)}) copy-start(s32[8]{0:T(128)} %param.26) | copy-start | bytes 100
  91.8 2.0 collective-permute-start.3
  91.9 2.6 %collective-permute-start.4 = (bf16[512,512]{1,0:T(8,128)(2,1)S(1)}, bf16[512,512]{1,0:T(8,128)(2,1)S(1)}, u32[]{:S(2)}, u32[]{:S(2)}) collective-permute-start(bf16[512,512]{1,0:T(8,128)(2,1)S(1)} %get-tuple-element.32), channel_id=1, source_target_pairs={{0,1},{1,0},{2,3},{3,2},{4,5},{5,4},{6,7},{7,6},{8,9},{9,8},{10,11... | collective-permute-start | bytes 1572872 | tf_op jit(solution)/shard_map/ppermute | solution.py:222
  96.6 14.3 %collective-permute-start.5 = (bf16[512,512]{1,0:T(8,128)(2,1)}, bf16[512,512]{1,0:T(8,128)(2,1)}, u32[]{:S(2)}, u32[]{:S(2)}) collective-permute-start(bf16[512,512]{1,0:T(8,128)(2,1)} %select_convert_fusion.1), channel_id=1, source_target_pairs={{0,2},{2,0},{1,3},{3,1},{4,6},{6,4},{5,7},{7,5},{8,10},{10,8},{9,1... | collective-permute-start | bytes 1572872 | tf_op jit(solution)/shard_map/ppermute | solution.py:231
  103.0 54.1 %all-to-all-start.2 = ((bf16[8,2,128,2,256]{4,3,2,1,0:T(2,128)(2,1)}), bf16[8,2,128,2,256]{4,3,2,1,0:T(2,128)(2,1)}, u32[]{:S(2)}, u32[]{:S(2)}) async-start(bf16[8,2,128,2,256]{4,3,2,1,0:T(2,128)(2,1)} %copy-done.1), calls=%async_computation.2 | async-start | bytes 4194304 | tf_op jit(solution)/shard_map/all_to_all | solution.py:312
  114.4 13.5 %collective-permute-start.6 = (bf16[512,512]{1,0:T(8,128)(2,1)}, bf16[512,512]{1,0:T(8,128)(2,1)}, u32[]{:S(2)}, u32[]{:S(2)}) collective-permute-start(bf16[512,512]{1,0:T(8,128)(2,1)} %add_convert_fusion.1), channel_id=1, source_target_pairs={{0,2},{2,0},{1,3},{3,1},{4,6},{6,4},{5,7},{7,5},{8,10},{10,8},{9,1... | collective-permute-start | bytes 1572872 | tf_op jit(solution)/shard_map/ppermute | solution.py:199
  114.9 31.4 %collective-permute-start.8 = (bf16[512,512]{1,0:T(8,128)(2,1)}, bf16[512,512]{1,0:T(8,128)(2,1)}, u32[]{:S(2)}, u32[]{:S(2)}) collective-permute-start(bf16[512,512]{1,0:T(8,128)(2,1)} %add_convert_fusion.1), channel_id=1, source_target_pairs={{0,1},{1,0},{2,3},{3,2},{4,5},{5,4},{6,7},{7,6},{8,9},{9,8},{10,11... | collective-permute-start | bytes 1572872 | tf_op jit(solution)/shard_map/ppermute | solution.py:200
  127.9 18.5 %collective-permute-start.7 = (bf16[512,512]{1,0:T(8,128)(2,1)}, bf16[512,512]{1,0:T(8,128)(2,1)}, u32[]{:S(2)}, u32[]{:S(2)}) collective-permute-start(bf16[512,512]{1,0:T(8,128)(2,1)} %collective-permute-done.6), channel_id=1, source_target_pairs={{0,1},{1,0},{2,3},{3,2},{4,5},{5,4},{6,7},{7,6},{8,9},{9,8},{10,11... | collective-permute-start | bytes 1572872 | tf_op jit(solution)/shard_map/ppermute | solution.py:201
  146.4 2.5 %copy-start.2 = (bf16[8,2,64,2,256]{4,3,2,1,0:T(2,128)(2,1)}, bf16[8,2,64,2,256]{4,3,2,1,0:T(2,128)(2,1)S(1)}, u32[]{:S(2)}) copy-start(bf16[8,2,64,2,256]{4,3,2,1,0:T(2,128)(2,1)S(1)} %regroup.3) | copy-start | bytes 3145732
  157.1 38.7 %all-to-all-start.3 = ((bf16[8,2,64,2,256]{4,3,2,1,0:T(2,128)(2,1)}), bf16[8,2,64,2,256]{4,3,2,1,0:T(2,128)(2,1)}, u32[]{:S(2)}, u32[]{:S(2)}) async-start(bf16[8,2,64,2,256]{4,3,2,1,0:T(2,128)(2,1)} %copy-done.2), calls=%async_computation.3 | async-start | bytes 2097152 | tf_op jit(solution)/shard_map/all_to_all | solution.py:328
  171.9 2.3 %collective-permute-start.9 = (bf16[512,512]{1,0:T(8,128)(2,1)}, bf16[512,512]{1,0:T(8,128)(2,1)}, u32[]{:S(2)}, u32[]{:S(2)}) collective-permute-start(bf16[512,512]{1,0:T(8,128)(2,1)} %get-tuple-element.27), channel_id=1, source_target_pairs={{0,1},{1,0},{2,3},{3,2},{4,5},{5,4},{6,7},{7,6},{8,9},{9,8},{10,11... | collective-permute-start | bytes 1572872 | tf_op jit(solution)/shard_map/ppermute | solution.py:222
  171.9 3.0 %collective-permute-start.10 = (bf16[512,512]{1,0:T(8,128)(2,1)}, bf16[512,512]{1,0:T(8,128)(2,1)}, u32[]{:S(2)}, u32[]{:S(2)}) collective-permute-start(bf16[512,512]{1,0:T(8,128)(2,1)} %get-tuple-element.26), channel_id=1, source_target_pairs={{0,1},{1,0},{2,3},{3,2},{4,5},{5,4},{6,7},{7,6},{8,9},{9,8},{10,11... | collective-permute-start | bytes 1572872 | tf_op jit(solution)/shard_map/ppermute | solution.py:222
  178.0 14.3 %collective-permute-start.11 = (bf16[512,512]{1,0:T(8,128)(2,1)}, bf16[512,512]{1,0:T(8,128)(2,1)}, u32[]{:S(2)}, u32[]{:S(2)}) collective-permute-start(bf16[512,512]{1,0:T(8,128)(2,1)} %select_convert_fusion), channel_id=1, source_target_pairs={{0,2},{2,0},{1,3},{3,1},{4,6},{6,4},{5,7},{7,5},{8,10},{10,8},{9,1... | collective-permute-start | bytes 1572872 | tf_op jit(solution)/shard_map/ppermute | solution.py:231
  (12 other events, 15.3 us)
